TPU v7x, 32 devices: a whole 2x2x4 slice. The times are simulated.
32 devices in a mesh: fsdp: 16 (over z, y, core), tp: 2 (over x).
Axes of the slice: x: 2, y: 2, z: 4, core: 2. Of those that a mesh axis runs over, the one named last changes fastest.
Arguments:
- tokens: bfloat16 [2, 16, 288, 2048], P(None, 'fsdp', 'tp'), may hold values from -6 to 6
- cotangent: bfloat16 [2, 16, 288, 2048], P(None, 'fsdp', 'tp'), may hold values from -6 to 6
- norm1_gain: bfloat16 [2048], replicated, may hold values from 0.5 to 1.5
- w_query: bfloat16 [2048, 4096], P('fsdp', 'tp'), may hold values from -0.125 to 0.125
- key_projection_weight: bfloat16 [2048, 512], P('fsdp', 'tp'), may hold values from -0.125 to 0.125
- value_projection_weight: bfloat16 [2048, 512], P('fsdp', 'tp'), may hold values from -0.125 to 0.125
- query_gain: bfloat16 [128], replicated, may hold values from 0.25 to 1.75
- key_gain: bfloat16 [128], replicated, may hold values from 0.25 to 1.75
- w_out: bfloat16 [4096, 2048], P('tp', 'fsdp'), may hold values from -0.375 to 0.375
- norm2_gain: bfloat16 [2048], replicated, may hold values from 0.5 to 1.5
- w_gate: bfloat16 [32, 2048, 768], P('fsdp', None, 'tp'), may hold values from -0.125 to 0.125
- w_up: bfloat16 [32, 2048, 768], P('fsdp', None, 'tp'), may hold values from -0.125 to 0.125
- w_down: bfloat16 [32, 768, 2048], P('fsdp', 'tp'), may hold values from -0.875 to 0.875
- routes: int32 [2, 16, 288, 8], P(None, 'fsdp'), may hold values from 0 to 31, all different within a row; in each aligned block of 288 rows (0 to 287, 288 to 575, ..., all dimensions but the last counted through in order) at most 84 rows name the same one
- gates: float32 [2, 16, 288, 8], P(None, 'fsdp'), may hold values from 0.06 to 0.2
Outputs:
- block_out: bfloat16 [2, 16, 288, 2048], P(None, 'fsdp', 'tp')
- input_grad: bfloat16 [2, 16, 288, 2048], P(None, 'fsdp', 'tp')
- norm1_grad: float32 [2048], replicated
- query_grad: float32 [2048, 4096], P('fsdp', 'tp')
- key_grad: float32 [2048, 512], P('fsdp', 'tp')
- value_grad: float32 [2048, 512], P('fsdp', 'tp')
- qnorm_grad: float32 [128], replicated
- knorm_grad: float32 [128], replicated
- out_proj_grad: float32 [4096, 2048], P('tp', 'fsdp')
- norm2_grad: float32 [2048], replicated
- gate_grad: float32 [32, 2048, 768], P('fsdp', None, 'tp')
- up_grad: float32 [32, 2048, 768], P('fsdp', None, 'tp')
- down_grad: float32 [32, 768, 2048], P('fsdp', 'tp')
Inputs may be any that keep to these rules, and one draw needn't show every extreme that they name: `routes`: A token names 8 different experts. The 288 tokens of one sequence in one micro-batch name each expert at most 84 times in all; in some sequences one expert is named exactly 84 times, and every expert is named somewhere.
All inputs are finite; a program needn't handle non-finite values.
Results may differ from a plain program's by a relative error of at most 0.02.
Values may be sent and summed in bfloat16 or wider, within the bound.
A program may use at most 512 MiB of HBM per device.

v0:
```python
import functools

import jax
import jax.numpy as jnp
from jax import lax
from jax.experimental import pallas as pl
from jax.experimental.pallas import tpu as pltpu
from jax.sharding import PartitionSpec as P

BLOCK = 256


EPSILON = 1e-06
ROPE_BASE = 1000000.0
MASKED = -1e30
TILE_PICKS = 128


def rms_scale(row_block, gain_row):
    return (
        row_block
        * lax.rsqrt(jnp.mean(row_block * row_block, axis=-1, keepdims=True) + EPSILON)
        * gain_row
    )


def rotary_tables(sequence_length, head_width):
    half_width = head_width // 2
    inverse = ROPE_BASE ** (-2.0 * jnp.arange(half_width, dtype=jnp.float32) / head_width)
    angles = jnp.arange(sequence_length, dtype=jnp.float32)[:, None] * inverse[None, :]
    cosine_table = jnp.concatenate([jnp.cos(angles), jnp.cos(angles)], axis=-1)[:, None, :]
    sine_values = jnp.concatenate([jnp.sin(angles), jnp.sin(angles)], axis=-1)[:, None, :]
    return (cosine_table, sine_values)


def rotate(head_rows, cosine_table, sine_values):
    half_width = head_rows.shape[-1] // 2
    turned = jnp.concatenate([-head_rows[..., half_width:], head_rows[..., :half_width]], axis=-1)
    return head_rows * cosine_table + turned * sine_values


def prepare_heads(projected, gain_row, cosine_table, sine_values):
    return rotate(rms_scale(projected, gain_row), cosine_table, sine_values)


def swiglu(gate_act, up_act):
    return jax.nn.silu(gate_act) * up_act


def slot_tables(route_rows, gate_rows, expert_count, capacity):
    sequence_length = route_rows.shape[0]
    top_count = route_rows.shape[1]
    pick_count = sequence_length * top_count
    tile_count = pick_count // TILE_PICKS
    flat_routes = route_rows.reshape(-1)
    onehot = (flat_routes[:, None] == jnp.arange(expert_count, dtype=jnp.int32)[None, :]).astype(
        jnp.bfloat16
    )
    tiles = onehot.reshape(tile_count, TILE_PICKS, expert_count)
    positions = jnp.arange(TILE_PICKS, dtype=jnp.int32)
    lower = (positions[None, :] < positions[:, None]).astype(jnp.bfloat16)
    within = jnp.einsum("ij,bje->bie", lower, tiles, preferred_element_type=jnp.float32)
    tile_totals = jnp.sum(tiles.astype(jnp.float32), axis=1)
    offsets = jnp.cumsum(tile_totals, axis=0) - tile_totals
    before = within + offsets[:, None, :]
    slot_rank = jnp.sum(before * tiles.astype(jnp.float32), axis=-1).reshape(-1).astype(jnp.int32)
    slot_index = flat_routes * capacity + slot_rank
    pick_ids = jnp.arange(pick_count, dtype=jnp.int32) // top_count
    slot_owner = (
        jnp.full((expert_count * capacity,), sequence_length, jnp.int32)
        .at[slot_index]
        .set(pick_ids)
    )
    slot_weight = (
        jnp.zeros((expert_count * capacity,), jnp.float32).at[slot_index].set(gate_rows.reshape(-1))
    )
    return (slot_index, slot_owner, slot_weight)


def exchanged_layer(
    tokens,
    cotangent,
    norm1_gain,
    w_query,
    key_projection_weight,
    value_projection_weight,
    query_gain,
    key_gain,
    w_out,
    norm2_gain,
    w_gate,
    w_up,
    w_down,
    routes,
    gates,
):
    batch_count = tokens.shape[0]
    model_width = tokens.shape[3]
    sequence_length = routes.shape[2]
    top_count = routes.shape[3]
    head_features = query_gain.shape[0]
    local_experts = w_gate.shape[0]
    fsdp_count = lax.axis_size("fsdp")
    all_experts = local_experts * fsdp_count
    capacity = 7 * top_count * sequence_length // (6 * all_experts)
    query_heads = w_query.shape[1] // head_features
    kv_heads = key_projection_weight.shape[1] // head_features
    group_size = query_heads // kv_heads
    score_scale = head_features ** (-0.5)
    cosine_table, sine_values = rotary_tables(sequence_length, head_features)
    block_ids = jnp.arange(sequence_length, dtype=jnp.int32) // BLOCK
    visible = (block_ids[None, :] <= block_ids[:, None])[None, None]
    first_gain = norm1_gain.astype(jnp.float32)
    second_gain = norm2_gain.astype(jnp.float32)
    query_factor_scale = query_gain.astype(jnp.float32)
    key_scale = key_gain.astype(jnp.float32)
    zero_row = jnp.zeros((1, model_width), jnp.bfloat16)
    buffer_shape = (fsdp_count, local_experts, capacity, model_width)

    def masked_scores(query_fourfold, key_rows):
        raw_scores = (
            jnp.einsum(
                "qcgd,kcd->cgqk", query_fourfold, key_rows, preferred_element_type=jnp.float32
            )
            * score_scale
        )
        return jnp.where(visible, raw_scores, MASKED)

    def prep_heads(projected, gain_row):
        return prepare_heads(projected, gain_row, cosine_table, sine_values)

    gain_sums = (
        jnp.zeros((model_width,), jnp.float32),
        jnp.zeros((model_width,), jnp.float32),
        jnp.zeros((head_features,), jnp.float32),
        jnp.zeros((head_features,), jnp.float32),
    )
    expert_grads = (
        jnp.zeros(w_gate.shape, jnp.float32),
        jnp.zeros(w_up.shape, jnp.float32),
        jnp.zeros(w_down.shape, jnp.float32),
    )
    attn_grads = tuple(
        (
            jnp.zeros(weight_part.shape, jnp.float32)
            for weight_part in (w_query, key_projection_weight, value_projection_weight, w_out)
        )
    )
    outputs = []
    input_grads = []
    for batch_index in range(batch_count):
        query_full, key_full, value_full, out_full = (
            lax.all_gather(w_query, "fsdp", axis=0, tiled=True),
            lax.all_gather(key_projection_weight, "fsdp", axis=0, tiled=True),
            lax.all_gather(value_projection_weight, "fsdp", axis=0, tiled=True),
            lax.all_gather(w_out, "fsdp", axis=1, tiled=True),
        )
        own_rows = tokens[batch_index, 0].astype(jnp.float32)
        own_cot = cotangent[batch_index, 0]
        route_rows = routes[batch_index, 0]
        gate_rows = gates[batch_index, 0]
        first_normed = rms_scale(own_rows, first_gain).astype(jnp.bfloat16)
        normed_all = lax.all_gather(first_normed, "tp", axis=0, tiled=True)
        query_projected = jnp.dot(
            normed_all, query_full, preferred_element_type=jnp.float32
        ).reshape(sequence_length, query_heads, head_features)
        key_projected = jnp.dot(normed_all, key_full, preferred_element_type=jnp.float32).reshape(
            sequence_length, kv_heads, head_features
        )
        value_row_list = (
            jnp.dot(normed_all, value_full, preferred_element_type=jnp.float32)
            .astype(jnp.bfloat16)
            .reshape(sequence_length, kv_heads, head_features)
        )
        query_rot = prep_heads(query_projected, query_factor_scale).astype(jnp.bfloat16)
        key_rot = prep_heads(key_projected, key_scale).astype(jnp.bfloat16)
        query_fourfold = query_rot.reshape(sequence_length, kv_heads, group_size, head_features)
        scores = masked_scores(query_fourfold, key_rot)
        row_max = jnp.max(scores, axis=-1, keepdims=True)
        exp_scores = jnp.exp(scores - row_max)
        totals = jnp.sum(exp_scores, axis=-1, keepdims=True)
        log_total = row_max + jnp.log(totals)
        prob_rows = (exp_scores / totals).astype(jnp.bfloat16)
        context = (
            jnp.einsum(
                "cgqk,kcd->qcgd", prob_rows, value_row_list, preferred_element_type=jnp.float32
            )
            .astype(jnp.bfloat16)
            .reshape(sequence_length, query_heads * head_features)
        )
        attn_own = lax.psum_scatter(
            jnp.dot(context, out_full, preferred_element_type=jnp.float32).astype(jnp.bfloat16),
            "tp",
            scatter_dimension=0,
            tiled=True,
        ).astype(jnp.float32)
        hidden_own = own_rows + attn_own
        second_normed = rms_scale(hidden_own, second_gain).astype(jnp.bfloat16)
        normed_two, cot_all = (
            lax.all_gather(second_normed, "tp", axis=0, tiled=True),
            lax.all_gather(own_cot, "tp", axis=0, tiled=True),
        )
        slot_index, slot_owner, slot_weight = slot_tables(
            route_rows, gate_rows, all_experts, capacity
        )
        padded_rows = jnp.concatenate([normed_two, zero_row], axis=0)
        send_rows = padded_rows[slot_owner].reshape(buffer_shape)
        expert_in = lax.all_to_all(send_rows, "fsdp", split_axis=0, concat_axis=0, tiled=True)
        gate_act = jnp.einsum(
            "sekd,edf->sekf", expert_in, w_gate, preferred_element_type=jnp.float32
        )
        up_act = jnp.einsum("sekd,edf->sekf", expert_in, w_up, preferred_element_type=jnp.float32)
        act_rows = swiglu(gate_act, up_act).astype(jnp.bfloat16)
        expert_out = jnp.einsum(
            "sekf,efd->sekd", act_rows, w_down, preferred_element_type=jnp.float32
        )
        returned = lax.all_to_all(
            expert_out.astype(jnp.bfloat16), "fsdp", split_axis=0, concat_axis=0, tiled=True
        ).astype(expert_out.dtype)
        picked = returned.reshape(all_experts * capacity, model_width)[slot_index].reshape(
            sequence_length, top_count, model_width
        )
        moe_part = jnp.sum(picked * gate_rows[:, :, None], axis=1)
        moe_own = lax.psum_scatter(
            moe_part.astype(jnp.bfloat16), "tp", scatter_dimension=0, tiled=True
        ).astype(jnp.float32)
        outputs.append((hidden_own + moe_own).astype(jnp.bfloat16))
        cot_padded = jnp.concatenate([cot_all, zero_row], axis=0)
        send_grads = (
            (slot_weight[:, None] * cot_padded[slot_owner])
            .astype(jnp.bfloat16)
            .reshape(buffer_shape)
        )
        out_grads = lax.all_to_all(send_grads, "fsdp", split_axis=0, concat_axis=0, tiled=True)
        act_grads = jnp.einsum(
            "sekd,efd->sekf", out_grads, w_down, preferred_element_type=jnp.float32
        )
        _, swiglu_back = jax.vjp(swiglu, gate_act, up_act)
        gate_grads, up_grads = swiglu_back(act_grads)
        gate_grads = gate_grads.astype(jnp.bfloat16)
        up_grads = up_grads.astype(jnp.bfloat16)
        expert_grads = (
            expert_grads[0]
            + jnp.einsum(
                "sekd,sekf->edf", expert_in, gate_grads, preferred_element_type=jnp.float32
            ),
            expert_grads[1]
            + jnp.einsum("sekd,sekf->edf", expert_in, up_grads, preferred_element_type=jnp.float32),
            expert_grads[2]
            + jnp.einsum("sekf,sekd->efd", act_rows, out_grads, preferred_element_type=jnp.float32),
        )
        input_part = jnp.einsum(
            "sekf,edf->sekd", gate_grads, w_gate, preferred_element_type=jnp.float32
        ) + jnp.einsum("sekf,edf->sekd", up_grads, w_up, preferred_element_type=jnp.float32)
        input_back = lax.all_to_all(
            input_part.astype(jnp.bfloat16), "fsdp", split_axis=0, concat_axis=0, tiled=True
        ).astype(input_part.dtype)
        normed_grads = jnp.sum(
            input_back.reshape(all_experts * capacity, model_width)[slot_index].reshape(
                sequence_length, top_count, model_width
            ),
            axis=1,
        )
        normed_own = lax.psum_scatter(
            normed_grads.astype(jnp.bfloat16), "tp", scatter_dimension=0, tiled=True
        ).astype(jnp.float32)
        _, second_back = jax.vjp(rms_scale, hidden_own, second_gain)
        hidden_part, second_gain_grad = second_back(normed_own)
        hidden_grad = own_cot.astype(jnp.float32) + hidden_part
        attn_grad_all = lax.all_gather(hidden_grad.astype(jnp.bfloat16), "tp", axis=0, tiled=True)
        out_weight_grad = jnp.einsum(
            "th,td->hd", context, attn_grad_all, preferred_element_type=jnp.float32
        )
        context_grad = (
            jnp.einsum("td,hd->th", attn_grad_all, out_full, preferred_element_type=jnp.float32)
            .astype(jnp.bfloat16)
            .reshape(sequence_length, kv_heads, group_size, head_features)
        )
        exp_again = jnp.exp(masked_scores(query_fourfold, key_rot) - log_total)
        probs_again = exp_again.astype(jnp.bfloat16)
        prob_grads = jnp.einsum(
            "qcgd,kcd->cgqk", context_grad, value_row_list, preferred_element_type=jnp.float32
        )
        value_grads = (
            jnp.einsum(
                "cgqk,qcgd->kcd", probs_again, context_grad, preferred_element_type=jnp.float32
            )
            .astype(jnp.bfloat16)
            .reshape(sequence_length, kv_heads * head_features)
        )
        score_grads = (
            exp_again * (prob_grads - jnp.sum(exp_again * prob_grads, axis=-1, keepdims=True))
        ).astype(jnp.bfloat16)
        query_rot_grads = (
            jnp.einsum("cgqk,kcd->qcgd", score_grads, key_rot, preferred_element_type=jnp.float32)
            * score_scale
        ).reshape(sequence_length, query_heads, head_features)
        key_rot_grads = (
            jnp.einsum(
                "cgqk,qcgd->kcd", score_grads, query_fourfold, preferred_element_type=jnp.float32
            )
            * score_scale
        )
        _, query_back = jax.vjp(prep_heads, query_projected, query_factor_scale)
        query_proj_grads, query_gain_grad = query_back(query_rot_grads)
        _, key_back = jax.vjp(prep_heads, key_projected, key_scale)
        key_proj_grads, key_gain_grad = key_back(key_rot_grads)
        query_proj_grads = query_proj_grads.astype(jnp.bfloat16).reshape(
            sequence_length, query_heads * head_features
        )
        key_proj_grads = key_proj_grads.astype(jnp.bfloat16).reshape(
            sequence_length, kv_heads * head_features
        )
        first_normed_grads = (
            jnp.einsum(
                "tq,dq->td", query_proj_grads, query_full, preferred_element_type=jnp.float32
            )
            + jnp.einsum("tq,dq->td", key_proj_grads, key_full, preferred_element_type=jnp.float32)
            + jnp.einsum("tq,dq->td", value_grads, value_full, preferred_element_type=jnp.float32)
        )
        weight_parts = (
            jnp.einsum(
                "td,tq->dq", normed_all, query_proj_grads, preferred_element_type=jnp.float32
            ),
            jnp.einsum("td,tq->dq", normed_all, key_proj_grads, preferred_element_type=jnp.float32),
            jnp.einsum("td,tq->dq", normed_all, value_grads, preferred_element_type=jnp.float32),
            out_weight_grad,
        )
        first_own = lax.psum_scatter(
            first_normed_grads.astype(jnp.bfloat16), "tp", scatter_dimension=0, tiled=True
        ).astype(jnp.float32)
        _, first_back = jax.vjp(rms_scale, own_rows, first_gain)
        row_part, first_gain_grad = first_back(first_own)
        input_grads.append((hidden_grad + row_part).astype(jnp.bfloat16))
        gain_sums = (
            gain_sums[0] + first_gain_grad,
            gain_sums[1] + second_gain_grad,
            gain_sums[2] + query_gain_grad,
            gain_sums[3] + key_gain_grad,
        )
        attn_grads = jax.tree.map(
            jnp.add,
            attn_grads,
            (
                lax.psum_scatter(weight_parts[0], "fsdp", scatter_dimension=0, tiled=True),
                lax.psum_scatter(weight_parts[1], "fsdp", scatter_dimension=0, tiled=True),
                lax.psum_scatter(weight_parts[2], "fsdp", scatter_dimension=0, tiled=True),
                lax.psum_scatter(weight_parts[3], "fsdp", scatter_dimension=1, tiled=True),
            ),
        )
    summed = lax.psum((gain_sums[0], gain_sums[1], gain_sums[2], gain_sums[3]), ("fsdp", "tp"))
    block_out = jnp.stack(outputs)[:, None]
    input_grad = jnp.stack(input_grads)[:, None]
    return (
        block_out,
        input_grad,
        summed[0],
        attn_grads[0],
        attn_grads[1],
        attn_grads[2],
        summed[2],
        summed[3],
        attn_grads[3],
        summed[1],
        expert_grads[0],
        expert_grads[1],
        expert_grads[2],
    )


MESH = pl.DeviceIdType.MESH
FSDP, TP = "fsdp", "tp"
PLANE = 4
LANES = 128
MIB = 1 << 20
RIGHT, LEFT, FIRST, SECOND, CORE, CROSS = range(6)
TRANSPOSED_LEFT = (((0,), (0,)), ((), ()))
TRANSPOSED_RIGHT = (((1,), (1,)), ((), ()))
OUTPUT, BACK = range(2)
CHUNK = 512


class Spot:
    def __init__(self, line, wide, turned=True):
        self.line = line
        self.wide = wide
        self.turned = turned
        self.planes = 4 if wide else 2
        index = lax.axis_index(FSDP)
        self.x = lax.axis_index(TP)
        self.z = lax.div(index, PLANE)
        self.y = lax.rem(lax.div(index, 2), 2)
        self.core = lax.rem(index, 2)

    def side(self, core, first, second):
        flip_y, flip_x = first, second
        if self.wide and self.turned:
            flip_y = (1 - core) * first + core * second
            flip_x = core * first + (1 - core) * second
        return self.y + flip_y * (1 - 2 * self.y), self.x + flip_x * (1 - 2 * self.x)

    def block(self, core, first, second, z):
        y, x = self.side(core, first, second)
        return z * PLANE + y * 2 + core, x

    def device(self, kind):
        if kind == RIGHT:
            return self.block(self.core, 0, 0, self.z + 1)
        if kind == LEFT:
            return self.block(self.core, 0, 0, self.z - 1)
        if kind == CORE:
            return self.block(1 - self.core, 0, 0, self.z)
        if kind == CROSS:
            return self.block(self.core, 0, 0, self.z)[0], 1 - self.x
        return self.block(self.core, int(kind == FIRST), int(kind == SECOND), self.z)

    def kinds(self):
        return (FIRST, SECOND, CORE) if self.wide else (FIRST, CORE)

    def number(self, first, second, z):
        return (second * 2 + first) * self.line + z

    def order(self, step):
        if isinstance(step, int) and step == 0:
            return [(self.z, None)]
        return [(self.z - step, self.z - step >= 0), (self.z + step, self.z + step < self.line)]

    def greet(self):
        barrier = pltpu.get_barrier_semaphore()

        def signal(kind):
            pl.semaphore_signal(barrier, inc=1, device_id=self.device(kind), device_id_type=MESH)

        for kind in self.kinds():
            signal(kind)
        when(self.z + 1 < self.line, lambda: signal(RIGHT))
        when(self.z > 0, lambda: signal(LEFT))
        around = (self.z + 1 < self.line).astype(jnp.int32) + (self.z > 0).astype(jnp.int32)
        pl.semaphore_wait(barrier, len(self.kinds()) + around)

    def send(self, source, target, send_sem, receive_sem, kind):
        return pltpu.make_async_remote_copy(
            src_ref=source,
            dst_ref=target,
            send_sem=send_sem,
            recv_sem=receive_sem,
            device_id=self.device(kind),
            device_id_type=MESH,
        )


def when(condition, action):
    def run():
        action()

    if condition is None or condition is True:
        run()
    elif condition is not False:
        pl.when(condition)(run)


class Spread:
    def __init__(self, spot, source, slot, send, receive, local):
        self.spot = spot
        self.slot = slot
        self.source = source
        self.sends = send
        self.receives = receive
        self.mine = pltpu.make_async_copy(source, slot(*spot.block(spot.core, 0, 0, spot.z)), local)

    def copy(self, first, second, z, kind, own=False):
        spot = self.spot
        place = self.slot(*spot.block(spot.core, first, second, z))
        number = spot.number(first, second, z)
        arrival = {
            RIGHT: number,
            LEFT: number,
            FIRST: spot.number(1, 0, z),
            SECOND: spot.number(first, 1, z),
            CORE: spot.planes * spot.line + number,
        }[kind]
        departure = {RIGHT: 0, LEFT: 1, FIRST: 2, SECOND: 3, CORE: 5}[kind] * spot.line + number
        source = self.source if own else place
        return spot.send(source, place, self.sends.at[departure], self.receives.at[arrival], kind)

    def arrived(self, first, second, z, other=False):
        spot = self.spot
        core = 1 - spot.core if other else spot.core
        place = self.slot(*spot.block(core, first, second, z))
        number = spot.number(first, second, z) + (spot.planes * spot.line if other else 0)
        spot.send(place, place, self.sends.at[0], self.receives.at[number], CORE).wait_recv()

    def steps(self):
        return self.spot.line + (3 if self.spot.wide else 1)

    def begin(self):
        spot = self.spot
        z = spot.z
        when(z + 1 < spot.line, lambda: self.copy(0, 0, z, RIGHT, True).start())
        when(z > 0, lambda: self.copy(0, 0, z, LEFT, True).start())
        for kind in spot.kinds():
            self.copy(0, 0, z, kind, True).start()
        self.mine.start()

    def step(self, step):
        spot = self.spot
        line, z = spot.line, spot.z

        def reached(away, action):
            inside = jnp.logical_and(away >= 0, away < line)
            when(jnp.logical_and(inside, z - away >= 0), lambda: action(z - away, True))
            when(
                jnp.logical_and(inside, jnp.logical_and(away > 0, z + away < line)),
                lambda: action(z + away, False),
            )

        def along(zz, from_left):
            self.arrived(0, 0, zz)
            if from_left:
                when(z + 1 < line, lambda: self.copy(0, 0, zz, RIGHT).start())
            else:
                when(z > 0, lambda: self.copy(0, 0, zz, LEFT).start())
            for kind in spot.kinds():
                self.copy(0, 0, zz, kind).start()

        def firsts(zz, _):
            self.arrived(1, 0, zz)
            if spot.wide:
                self.copy(1, 0, zz, SECOND).start()
            self.copy(1, 0, zz, CORE).start()

        def lasts(first):
            def action(zz, _):
                self.arrived(first, 1, zz)
                self.copy(first, 1, zz, CORE).start()

            return action

        step = jnp.asarray(step, jnp.int32)
        reached(step, along)
        reached(step - 1, firsts)
        if spot.wide:
            reached(step - 2, lasts(0))
            reached(step - 3, lasts(1))

    def finish(self):
        spot = self.spot
        z = spot.z

        def body(zz, _):
            when(
                jnp.logical_and(z + 1 < spot.line, zz <= z),
                lambda: self.copy(0, 0, zz, RIGHT).wait_send(),
            )
            when(jnp.logical_and(z > 0, zz >= z), lambda: self.copy(0, 0, zz, LEFT).wait_send())
            self.copy(0, 0, zz, FIRST).wait_send()
            for second in range(2 if spot.wide else 1):
                for first in (0, 1):
                    if spot.wide and not second:
                        self.copy(first, 0, zz, SECOND).wait_send()
                    self.copy(first, second, zz, CORE).wait_send()
                    self.arrived(first, second, zz, other=True)
            return 0

        lax.fori_loop(0, spot.line, body, 0)
        self.mine.wait()


class LateSpread(Spread):
    def steps(self):
        return self.spot.line + 2

    def copy(self, first, second, z, kind, own=False):
        spot = self.spot
        place = self.slot(*spot.block(spot.core, first, second, z))
        number = spot.number(first, second, z)
        arrival = {
            RIGHT: number,
            LEFT: number,
            FIRST: spot.number(1, 0, z),
            SECOND: spot.number(first, 1, z),
            CORE: spot.planes * spot.line + number,
        }[kind]
        departure = {RIGHT: 0, LEFT: 4, CORE: 8, FIRST: 12, SECOND: 13}[kind] * spot.line + number
        source = self.source if own else place
        return spot.send(source, place, self.sends.at[departure], self.receives.at[arrival], kind)

    def along_both(self, first, second, own=False):
        spot = self.spot
        z = spot.z
        when(z + 1 < spot.line, lambda: self.copy(first, second, z, RIGHT, own).start())
        when(z > 0, lambda: self.copy(first, second, z, LEFT, own).start())
        self.copy(first, second, z, CORE, own).start()

    def begin(self):
        self.copy(0, 0, self.spot.z, FIRST, True).start()
        self.copy(0, 0, self.spot.z, SECOND, True).start()
        self.along_both(0, 0, True)
        self.mine.start()

    def step(self, step):
        spot = self.spot
        line, z = spot.line, spot.z
        step = jnp.asarray(step, jnp.int32)

        def passed(first, second, zz, kind, more):
            self.arrived(first, second, zz)
            when(more, lambda: self.copy(first, second, zz, kind).start())
            self.copy(first, second, zz, CORE).start()

        for first, second in ((0, 0), (1, 0), (0, 1), (1, 1)):
            away = step - (first + second)

            def here():
                self.arrived(first, second, z)
                if first and not second:
                    self.copy(1, 0, z, SECOND).start()
                self.along_both(first, second)

            if first or second:
                when(away == 0, here)
            far = jnp.logical_and(away > 0, away < line)
            when(
                jnp.logical_and(far, z - away >= 0),
                lambda: passed(first, second, z - away, RIGHT, z + 1 < line),
            )
            when(
                jnp.logical_and(far, z + away < line),
                lambda: passed(first, second, z + away, LEFT, z > 0),
            )

    def finish(self):
        spot = self.spot
        z = spot.z

        def body(zz, _):
            for second in (0, 1):
                for first in (0, 1):
                    when(
                        jnp.logical_and(z + 1 < spot.line, zz <= z),
                        lambda: self.copy(first, second, zz, RIGHT).wait_send(),
                    )
                    when(
                        jnp.logical_and(z > 0, zz >= z),
                        lambda: self.copy(first, second, zz, LEFT).wait_send(),
                    )
                    self.copy(first, second, zz, CORE).wait_send()
                    self.arrived(first, second, zz, other=True)
            return 0

        lax.fori_loop(0, spot.line, body, 0)
        self.copy(0, 0, z, FIRST).wait_send()
        for first in (0, 1):
            self.copy(first, 0, z, SECOND).wait_send()
        self.mine.wait()


def rows_spread(spot, source, place, rows, semaphores, at):
    late = late_rows(rows)
    early = rows - late
    send, receive, late_send, late_receive, local = semaphores

    def slot(start, size):
        return lambda block, side: place(block, side * rows + start, size)

    return [
        Spread(
            spot,
            source.at[pl.ds(0, early)],
            slot(0, early),
            send.at[at],
            receive.at[at],
            local.at[at, 0],
        ),
        LateSpread(
            spot,
            source.at[pl.ds(early, late)],
            slot(early, late),
            late_send.at[at],
            late_receive.at[at],
            local.at[at, 1],
        ),
    ]


def late_rows(rows):
    return max(16, round(rows * 2 / 9 / 16) * 16)


def rows_semaphores(batch, line):
    counts = (*spread_count(line, True), 15 * line, 8 * line, 2)
    return [pltpu.SemaphoreType.DMA((batch, count)) for count in counts]


def run_trees(trees):
    for tree in trees:
        tree.begin()

    def body(step, _):
        for tree in trees:
            tree.step(step)
        return 0

    lax.fori_loop(1, max(tree.steps() for tree in trees), body, 0)
    for tree in trees:
        tree.finish()


def spread_count(line, wide):
    return (9 if wide else 7) * line, (8 if wide else 4) * line


def mingle(work, others):
    for index, piece in enumerate(work):
        piece()
        for other in others[
            index * len(others) // len(work) : (index + 1) * len(others) // len(work)
        ]:
            other()


def rows_at(ref, index, size):
    return ref.at[pl.ds(pl.multiple_of(index * size, 16), size)]


def columns_at(ref, index, size):
    return ref.at[:, pl.ds(pl.multiple_of(index * size, LANES), size)]


def norm_rows(target, source, gain):
    def body(step, _):
        rows = pl.ds(pl.multiple_of(step * 16, 16), 16)
        value = source[rows, :].astype(jnp.float32)
        target[rows, :] = rms_scale(value, gain[...].astype(jnp.float32)).astype(target.dtype)
        return 0

    lax.fori_loop(0, target.shape[0] // 16, body, 0)


def turned_heads(value, gain, cosine, sine):
    normed = rms_scale(value, gain)
    return normed * cosine + pltpu.roll(normed, normed.shape[-1] // 2, 1) * sine


def visible_blocks(length, group):
    blocks = []
    for start in range(0, length, BLOCK):
        stop = min(start + BLOCK, length)
        heads = max(1, BLOCK // (stop - start))
        while group % heads:
            heads -= 1
        blocks.append((start, stop, stop, heads))
    return blocks


def softmax(scores):
    raised = jnp.exp(scores - jnp.max(scores, axis=0, keepdims=True))
    return raised * (1.0 / jnp.sum(raised, axis=0, keepdims=True))


def for_heads(low, high, heads, body):
    turns = 2 if heads == 1 and (high - low) % 2 == 0 else 1

    def turn(step, _):
        for i in range(turns):
            body(low + (step * turns + i) * heads)
        return 0

    count = (high - low) // (heads * turns)
    if count == 1:
        turn(0, 0)
    else:
        lax.fori_loop(0, count, turn, 0)


def head_columns(head, features):
    return pl.ds(pl.multiple_of(head * features, LANES), features)


def forward_kernel(
    line,
    heads,
    kv_heads,
    tokens_ref,
    cot_ref,
    in_ref,
    out_ref,
    picks_ref,
    gain1_ref,
    gain2_ref,
    query_gain_ref,
    key_gain_ref,
    cosine_ref,
    sine_ref,
    cot_all,
    in_all,
    out_all,
    picks_all,
    normed_all,
    projected_all,
    context_all,
    hidden_all,
    second_all,
    in_w,
    out_w,
    tokens,
    normed,
    projected,
    context,
    queries,
    keys,
    values,
    mixed,
    mixed_other,
    hidden,
    second,
    narrow_send,
    narrow_receive,
    cot_send,
    cot_receive,
    cot_late_send,
    cot_late_receive,
    cot_local,
    local,
    token_send,
    token_receive,
    mixed_send,
    mixed_receive,
    save_sem,
):
    cot_semaphores = (cot_send, cot_receive, cot_late_send, cot_late_receive, cot_local)
    batch, half, width = tokens_ref.shape
    length = 2 * half
    depth, out_width = in_ref.shape[0], out_ref.shape[1]
    features = query_gain_ref.shape[1]
    narrow = Spot(line, False)
    spot = Spot(line, True, turned=False)
    x = spot.x
    spot.greet()
    slots = [
        (picks_ref, lambda block, side: picks_all.at[block]),
        (in_ref, lambda block, side: rows_at(in_w, block, depth)),
        (out_ref, lambda block, side: columns_at(out_w, block, out_width)),
    ]
    weights = [
        Spread(narrow, source, slot, narrow_send.at[i], narrow_receive.at[i], local.at[i])
        for i, (source, slot) in enumerate(slots)
    ]
    place = lambda block, start, size: cot_all.at[block, pl.ds(pl.multiple_of(start, 16), size)]
    cots = rows_spread(spot, cot_ref.at[0], place, half, cot_semaphores, 0)
    early, late = weights[:2], weights[2]
    for tree in early:
        tree.begin()

    def token_copies(i):
        place = rows_at(tokens.at[i], x, half)
        return (
            pltpu.make_async_copy(tokens_ref.at[i], place, local.at[3 + i]),
            spot.send(tokens_ref.at[i], place, token_send.at[i], token_receive.at[i], CROSS),
        )

    for i in range(batch):
        for copy in token_copies(i):
            copy.start()
    def steps(step, _):
        for tree in early:
            tree.step(step)
        return 0

    lax.fori_loop(1, late.steps(), steps, 0)
    late.begin()
    for tree in cots:
        tree.begin()
    for i in range(batch):
        mine, other = token_copies(i)
        mine.wait()
        other.wait_send()
        place = rows_at(tokens.at[i], 1 - x, half)
        spot.send(place, place, token_send.at[i], token_receive.at[i], CROSS).wait_recv()
    for i in range(batch):
        norm_rows(normed.at[i], tokens.at[i], gain1_ref)
    for tree in early:
        tree.finish()

    def save(source, target, index):
        return pltpu.make_async_copy(source, target, save_sem.at[index])

    saves = [save(in_w, in_all, 0), save(out_w, out_all, 1)]
    saves[0].start()

    def project(i, start, stop):
        for at in range(start, stop, CHUNK):
            projected[i, :, at : at + CHUNK] = jnp.dot(
                normed[i], in_w[:, at : at + CHUNK], preferred_element_type=jnp.float32
            )

    scale = features ** (-0.5)

    group = heads // kv_heads

    def prepare_keys(i):
        base = heads * features
        for head in range(kv_heads):
            at = base + head * features
            keys[head] = turned_heads(
                projected[i, :, at : at + features],
                key_gain_ref[...].astype(jnp.float32),
                cosine_ref[...],
                sine_ref[...],
            ).astype(jnp.bfloat16)
            at = base + (kv_heads + head) * features
            values[head] = projected[i, :, at : at + features].astype(jnp.bfloat16)

    def prepare_queries(i, shared):
        def prepare(member):
            columns = head_columns(shared * group + member, features)
            queries[member] = turned_heads(
                projected[i, :, columns], query_gain_ref[...].astype(jnp.float32), cosine_ref[...], sine_ref[...]
            ).astype(jnp.bfloat16)

        for_heads(0, group, 1, prepare)

    def attend(i, shared, start, stop, seen, at_once, low, high):
        count = stop - start

        def block(member):
            query = queries[pl.ds(member, at_once), start:stop, :].reshape(-1, features)
            scores = lax.dot_general(
                keys[shared, :seen, :],
                query,
                TRANSPOSED_RIGHT,
                preferred_element_type=jnp.float32,
            )
            rows = lax.dot_general(
                softmax(scores * scale).astype(jnp.bfloat16),
                values[shared, :seen, :],
                TRANSPOSED_LEFT,
                preferred_element_type=jnp.float32,
            ).astype(jnp.bfloat16)
            for j in range(at_once):
                columns = head_columns(shared * group + member + j, features)
                context[i, start:stop, columns] = rows[j * count : (j + 1) * count]

        for_heads(low, high, at_once, block)

    def mixed_copy(i):
        return spot.send(
            rows_at(mixed.at[i], 1 - x, half),
            mixed_other.at[i],
            mixed_send.at[i],
            mixed_receive.at[i],
            CROSS,
        )

    def mix(i, start, stop):
        for at in range(start, stop, CHUNK):
            mixed[i, :, at : at + CHUNK] = jnp.dot(
                context[i], out_w[:, at : at + CHUNK], preferred_element_type=jnp.float32
            ).astype(jnp.bfloat16)
        if stop == width:
            mixed_copy(i).start()

    def close(i):
        mixed_copy(i).wait()
        add_rows(
            hidden.at[i],
            [rows_at(tokens.at[i], x, half), rows_at(mixed.at[i], x, half), mixed_other.at[i]],
        )
        norm_rows(second.at[i], hidden.at[i], gain2_ref)

    def late_done():
        late.finish()
        saves[1].start()

    def steps_of(trees, low, high):
        return [
            functools.partial(tree.step, step)
            for step in range(low, high)
            for tree in trees
            if step < tree.steps()
        ]

    in_width = in_w.shape[1]
    parts = lambda size: [(at, min(at + 2 * CHUNK, size)) for at in range(0, size, 2 * CHUNK)]
    opening, middle, closing = [], [], []
    for i in range(batch):
        opening += [functools.partial(project, i, *part) for part in parts(in_width)]
        middle.append(functools.partial(prepare_keys, i))
        for shared in range(kv_heads):
            middle.append(functools.partial(prepare_queries, i, shared))
            for start, stop, seen, at_once in visible_blocks(length, group):
                share = max(at_once, group // 2)
                for low in range(0, group, share):
                    middle.append(
                        functools.partial(
                            attend, i, shared, start, stop, seen, at_once, low, low + share
                        )
                    )
        closing += [functools.partial(mix, i, *part) for part in parts(width)]
    closing += [functools.partial(close, i) for i in range(batch)]
    last = cots[0].steps()
    mingle(opening + middle, steps_of([late] + cots, 1, last))
    late_done()
    for piece in closing:
        piece()

    saves += [
        save(source, target, 2 + i)
        for i, (source, target) in enumerate(
            [
                (normed, normed_all),
                (projected, projected_all),
                (context, context_all),
                (hidden, hidden_all),
                (second, second_all),
            ]
        )
    ]
    for copy in saves[2:]:
        copy.start()
    for tree in cots:
        tree.finish()
    for copy in saves:
        copy.wait()


def run_forward(tokens, cot, weight_in, weight_out, picks, gains, tables, fsdp_count, kv_heads):
    line = fsdp_count // PLANE
    batch, half, width = tokens.shape
    length = 2 * half
    features = gains[2].shape[1]
    heads = weight_out.shape[0] // features
    in_shape = (weight_in.shape[0] * fsdp_count, weight_in.shape[1])
    out_shape = (weight_out.shape[0], weight_out.shape[1] * fsdp_count)
    narrow = spread_count(line, False)
    anywhere = pl.BlockSpec(memory_space=pl.ANY)
    inside = pl.BlockSpec(memory_space=pltpu.VMEM)
    shape = lambda dims, kind=jnp.bfloat16: jax.ShapeDtypeStruct(dims, kind)
    vmem = lambda *dims: pltpu.VMEM(dims, jnp.bfloat16)
    sem = lambda *dims: pltpu.SemaphoreType.DMA(dims)
    kept = (
        ((batch, length, width), jnp.bfloat16),
        ((batch, length, weight_in.shape[1]), jnp.float32),
        ((batch, length, heads * features), jnp.bfloat16),
        ((batch, half, width), jnp.float32),
        ((batch, half, width), jnp.bfloat16),
    )
    return pl.pallas_call(
        functools.partial(forward_kernel, line, heads, kv_heads),
        out_shape=(
            shape((fsdp_count, length, width)),
            shape(in_shape),
            shape(out_shape),
            shape((fsdp_count, *picks.shape), picks.dtype),
            *(shape(*one) for one in kept),
        ),
        in_specs=[anywhere] * 5 + [inside] * 6,
        out_specs=(anywhere,) * 9,
        scratch_shapes=[
            vmem(*in_shape),
            vmem(*out_shape),
            vmem(batch, length, width),
            *(pltpu.VMEM(*one) for one in kept[:3]),
            vmem(heads // kv_heads, length, features),
            vmem(kv_heads, length, features),
            vmem(kv_heads, length, features),
            vmem(batch, length, width),
            vmem(batch, half, width),
            *(pltpu.VMEM(*one) for one in kept[3:]),
            sem(3, narrow[0]),
            sem(3, narrow[1]),
            *rows_semaphores(1, line),
            sem(3 + batch),
            sem(batch),
            sem(batch),
            sem(batch),
            sem(batch),
            sem(7),
        ],
        compiler_params=pltpu.CompilerParams(
            collective_id=1, has_side_effects=True, vmem_limit_bytes=60 * MIB
        ),
    )(tokens, cot, weight_in, weight_out, picks, *gains, *tables)


def add_rows(target, sources):
    def body(step, _):
        rows = pl.ds(pl.multiple_of(step * 16, 16), 16)
        total = sources[0][rows, :].astype(jnp.float32)
        for source in sources[1:]:
            total = total + source[rows, :].astype(jnp.float32)
        target[rows, :] = total.astype(target.dtype)
        return 0

    lax.fori_loop(0, target.shape[0] // 16, body, 0)


class Collect:
    def __init__(self, spot, part, total, cores, firsts, rights, lefts, send, receive):
        self.spot = spot
        self.part = part
        self.total = total
        self.places = {CORE: cores, FIRST: firsts, RIGHT: rights, LEFT: lefts}
        line = spot.line
        self.base = {CORE: 0, FIRST: 2 * line, RIGHT: 3 * line, LEFT: 4 * line}
        self.sends = send
        self.receives = receive

    def own(self, first, z):
        return self.part(*self.spot.block(self.spot.core, first, 0, z))

    def copy(self, kind, first, z):
        spot = self.spot
        number = first * spot.line + z if kind == CORE else z
        source = self.part(*spot.block(1 - spot.core, first, 0, z)) if kind == CORE else self.own(first, z)
        at = self.base[kind] + number
        return spot.send(
            source, self.places[kind].at[number], self.sends.at[at], self.receives.at[at], kind
        )

    def arrived(self, kind, number):
        place = self.places[kind].at[number]
        at = self.base[kind] + number
        self.spot.send(place, place, self.sends.at[0], self.receives.at[at], CORE).wait_recv()
        return place

    def begin(self, z):
        for first in (1, 0):
            self.copy(CORE, first, z).start()

    def to_first(self, z):
        add_rows(self.own(1, z), [self.own(1, z), self.arrived(CORE, self.spot.line + z)])
        self.copy(FIRST, 1, z).start()

    def summands(self, z):
        return [self.own(0, z), self.arrived(CORE, z), self.arrived(FIRST, z)]

    def cross(self):
        for step in reversed(range(self.spot.line)):
            for zz, valid in self.spot.order(step):
                when(valid, functools.partial(self.to_first, zz))

    def onward(self, kind, zz):
        spot = self.spot
        sources = self.summands(zz)
        target = self.own(0, zz)
        behind = spot.z > 0 if kind == RIGHT else spot.z + 1 < spot.line
        when(behind, lambda: add_rows(target, sources + [self.arrived(kind, zz)]))
        when(jnp.logical_not(behind), lambda: add_rows(target, sources))
        self.copy(kind, 0, zz).start()

    def last(self):
        z, line = self.spot.z, self.spot.line
        sources = self.summands(z)

        def end(kinds):
            add_rows(self.total, sources + [self.arrived(kind, z) for kind in kinds])

        when(z == 0, lambda: end([LEFT]))
        when(z == line - 1, lambda: end([RIGHT]))
        when(jnp.logical_and(z > 0, z < line - 1), lambda: end([RIGHT, LEFT]))

    def finish(self):
        spot = self.spot
        for zz in range(spot.line):
            for first in (0, 1):
                self.copy(CORE, first, zz).wait_send()
            self.copy(FIRST, 1, zz).wait_send()
            when(zz > spot.z, lambda: self.copy(RIGHT, 0, zz).wait_send())
            when(zz < spot.z, lambda: self.copy(LEFT, 0, zz).wait_send())

    def tasks(self):
        spot = self.spot
        work = []
        for step in reversed(range(1, spot.line)):
            for kind, (zz, valid) in zip((LEFT, RIGHT), spot.order(step)):
                action = functools.partial(self.onward, kind, zz)
                work.append(functools.partial(when, valid, action))
        return work + [self.last, self.finish]


def collect_scratch(line, shape):
    counts = (2 * line, line, line, line)
    return [pltpu.VMEM((count, *shape), jnp.bfloat16) for count in counts] + [
        pltpu.SemaphoreType.DMA((5 * line,)),
        pltpu.SemaphoreType.DMA((5 * line,)),
    ]


BOXES = 6


def plane_in_turn(line, group):
    turn = lax.rem(group, line)
    step = lax.div(turn, 2)
    return jnp.where(lax.rem(turn, 2) == 0, step, line - 1 - step)


class Sums:
    def __init__(self, spot, parts, cores, places, inbox, outbox, semaphores, plane, inside, ready, done, turns):
        self.spot = spot
        self.parts = parts
        self.cores = cores
        self.seconds, self.firsts, self.ends = places
        self.inbox = inbox
        self.outbox = outbox
        (
            self.inbox_sem,
            self.outbox_sem,
            self.second_receive,
            self.first_receive,
            self.end_receive,
        ) = semaphores
        self.plane = plane
        self.inside = inside
        self.ready = ready
        self.done = done
        self.turns = turns

    def second_slot(self, turn, first):
        return turn * 2 + first

    def first_slot(self, turn):
        return 2 * self.turns + turn

    def end_slot(self, turn, kind):
        return 3 * self.turns + turn * 2 + kind

    def free(self, unit, turn, first):
        pass

    def second_send(self, unit, turn, first):
        slot = self.second_slot(turn, first)
        return self.spot.send(
            self.outbox.at[slot],
            self.seconds.at[unit, first],
            self.outbox_sem.at[slot],
            self.second_receive.at[unit, first],
            SECOND,
        )

    def first_send(self, unit, turn):
        slot = self.first_slot(turn)
        return self.spot.send(
            self.outbox.at[slot],
            self.firsts.at[unit],
            self.outbox_sem.at[slot],
            self.first_receive.at[unit],
            FIRST,
        )

    def end_send(self, unit, turn, kind):
        slot = self.end_slot(turn, kind)
        return self.spot.send(
            self.outbox.at[slot],
            self.ends.at[unit, kind],
            self.outbox_sem.at[slot],
            self.end_receive.at[unit, kind],
            kind,
        )

    def received(self, place, semaphore):
        self.spot.send(place, place, self.outbox_sem.at[0], semaphore, CORE).wait_recv()

    def sources(self, unit, first, second):
        y, x = self.spot.side(self.spot.core, first, second)
        half = self.inbox.shape[1]
        return [rows_at(self.parts(unit, y), x, half), rows_at(self.cores(unit, y), x, half)]

    def summands(self, unit):
        return self.sources(unit, 0, 0) + [self.seconds.at[unit, 0], self.firsts.at[unit]]

    def load(self, source, slot):
        return pltpu.make_async_copy(source, self.inbox.at[slot], self.inbox_sem.at[slot])

    def add(self, target, base, numbers):
        add_rows(target, [self.inbox.at[base + i] for i in numbers])

    def end_roles(self, half_step, delay):
        z, line = self.spot.z, self.spot.line
        unit = half_step - 3 - delay
        valid = self.inside(unit)
        plane = self.plane(unit)
        right = jnp.logical_and(valid, jnp.logical_and(z < plane, delay == z))
        left = jnp.logical_and(valid, jnp.logical_and(z > plane, delay == line - 1 - z))
        last = jnp.logical_and(
            valid,
            jnp.logical_and(z == plane, delay == jnp.maximum(plane, line - 1 - plane)),
        )
        return unit, right, left, last

    def end_task(self, half_step, delay, parity):
        z, line = self.spot.z, self.spot.line
        turn = (parity - 3 - delay) % self.turns
        unit, right, left, last = self.end_roles(half_step, delay)
        some = jnp.logical_or(right, jnp.logical_or(left, last))
        from_left = jnp.logical_and(jnp.logical_or(right, last), z > 0)
        from_right = jnp.logical_and(jnp.logical_or(left, last), z + 1 < line)
        present = ((RIGHT, from_left), (LEFT, from_right))

        def fetch(base):
            def action():
                self.received(self.seconds.at[unit, 0], self.second_receive.at[unit, 0])
                self.received(self.firsts.at[unit], self.first_receive.at[unit])
                for i, source in enumerate(self.summands(unit)):
                    self.load(source, base + i).start()
                for kind, there in present:

                    def arrive():
                        self.received(self.ends.at[unit, kind], self.end_receive.at[unit, kind])
                        self.load(self.ends.at[unit, kind], base + 4 + kind).start()

                    when(there, arrive)

            when(some, action)

        def add(base):
            def action():
                for i, source in enumerate(self.summands(unit)):
                    self.load(source, base + i).wait()
                for kind, there in present:
                    when(there, lambda: self.load(self.ends.at[unit, kind], base + 4 + kind).wait())
                numbers = list(range(4))
                for kind, chosen, behind in ((RIGHT, right, z > 0), (LEFT, left, z + 1 < line)):

                    def onward():
                        target = self.outbox.at[self.end_slot(turn, kind)]
                        self.free(unit, turn, 0)
                        when(behind, lambda: self.add(target, base, numbers + [4 + kind]))
                        when(jnp.logical_not(behind), lambda: self.add(target, base, numbers))
                        self.end_send(unit, turn, kind).start()

                    when(chosen, onward)

                def finish():
                    def into(target):
                        both = jnp.logical_and(from_left, from_right)
                        when(both, lambda: self.add(target, base, numbers + [4, 5]))
                        for kind, there in present:
                            when(
                                jnp.logical_and(there, jnp.logical_not(both)),
                                lambda: self.add(target, base, numbers + [4 + kind]),
                            )

                    self.done(unit, turn, into)

                when(last, finish)

            when(some, action)

        return fetch, add

    def retire(self, half_step, parity):
        before = half_step - self.turns
        now, then = (parity - 1) % self.turns, (parity - 2) % self.turns
        when(
            self.inside(before - 1),
            lambda: [self.second_send(before - 1, now, first).wait_send() for first in range(2)],
        )
        when(self.inside(before - 2), lambda: self.first_send(before - 2, then).wait_send())
        for delay in range(self.spot.line):
            if self.inside(before - 3 - delay) is False:
                continue
            unit, right, left, _ = self.end_roles(before, delay)
            turn = (parity - 3 - delay) % self.turns
            when(right, lambda: self.end_send(unit, turn, RIGHT).wait_send())
            when(left, lambda: self.end_send(unit, turn, LEFT).wait_send())

    def simple_task(self, valid, ready, inputs, slot, send, free=lambda: None):
        def fetch(base):
            ready()

            def action():
                for i, source in enumerate(inputs()):
                    self.load(source, base + i).start()

            when(valid, action)

        def add(base):
            def action():
                refs = inputs()
                for i, source in enumerate(refs):
                    self.load(source, base + i).wait()
                free()
                self.add(self.outbox.at[slot], base, range(len(refs)))
                send().start()

            when(valid, action)

        return fetch, add

    def tasks(self, half_step, parity):
        one, two = half_step - 1, half_step - 2
        now, then = (parity - 1) % self.turns, (parity - 2) % self.turns
        tasks = [
            self.second_task(one, now, 1, functools.partial(self.ready, one)),
            self.second_task(one, now, 0, lambda: None),
            self.first_task(two, then),
        ]
        for delay in range(self.spot.line):
            if self.inside(half_step - 3 - delay) is not False:
                tasks.append(self.end_task(half_step, delay, parity))
        return tasks

    def second_task(self, unit, turn, first, ready):
        return self.simple_task(
            self.inside(unit),
            ready,
            lambda: self.sources(unit, first, 1),
            self.second_slot(turn, first),
            lambda: self.second_send(unit, turn, first),
        )

    def first_task(self, unit, turn):
        arrive = lambda: self.received(self.seconds.at[unit, 1], self.second_receive.at[unit, 1])

        def send():
            return self.first_send(unit, turn)

        return self.simple_task(
            self.inside(unit),
            lambda: when(self.inside(unit), arrive),
            lambda: self.sources(unit, 1, 0) + [self.seconds.at[unit, 1]],
            self.first_slot(turn),
            send,
            lambda: self.free(unit, turn, 1),
        )

    def weave(self, tasks, pieces):
        buffers = self.inbox.shape[0] // BOXES
        if buffers > 1:
            tasks[0][0](0)
        for index, (fetch, add) in enumerate(tasks):
            if buffers == 1:
                fetch(0)
            elif index + 1 < len(tasks):
                tasks[index + 1][0]((index + 1) % 2 * BOXES)
            share = -(-len(pieces) // (len(tasks) - index))
            for piece in pieces[:share]:
                piece()
            pieces = pieces[share:]
            add(index % buffers * BOXES)

    def half_steps(self, units):
        return units + self.spot.line + 2


def norm_back(value, grads, gain):
    scale = lax.rsqrt(jnp.mean(value * value, axis=-1, keepdims=True) + EPSILON)
    unit = value * scale
    scaled = grads * gain
    back = scale * (scaled - unit * jnp.mean(scaled * unit, axis=-1, keepdims=True))
    return back, grads * unit


def backward_kernel(
    line,
    heads,
    kv_heads,
    cot_ref,
    totals_ref,
    hidden_ref,
    projected_ref,
    context_ref,
    in_ref,
    out_ref,
    tokens_ref,
    gain1_ref,
    gain2_ref,
    query_gain_ref,
    key_gain_ref,
    cosine_ref,
    sine_ref,
    block_out,
    input_grad,
    grads_all,
    out_total,
    gain_grads,
    elements,
    cots,
    tokens,
    kept,
    result,
    context,
    hidden_grads,
    context_grads,
    grads,
    normed_other,
    weight_rows,
    queries_f,
    shared_f,
    queries,
    query_grads,
    sums,
    out_grads,
    cores,
    firsts,
    rights,
    lefts,
    tree_send,
    tree_receive,
    load_sem,
    row_sem,
    head_sem,
    save_sem,
    hidden_send,
    hidden_receive,
    normed_send,
    normed_receive,
):
    batch, half, width = cot_ref.shape
    length = 2 * half
    features = query_gain_ref.shape[1]
    group = heads // kv_heads
    base = heads * features
    out_width = out_total.shape[1]
    narrow, spot = Spot(line, False), Spot(line, True)
    x = spot.x
    scale = features ** (-0.5)
    normed_grads = context_grads

    def load(source, target, index):
        return pltpu.make_async_copy(source, target, load_sem.at[index])

    def element_loads(i):
        return [
            load(hidden_ref.at[i], elements.at[0], 0),
            load(totals_ref.at[i, BACK], elements.at[1], 1),
            load(totals_ref.at[i, OUTPUT], elements.at[2], 2),
        ]

    first_loads = [load(cot_ref, cots, 3), load(tokens_ref, tokens, 4)] + [
        load(context_ref.at[i], rows_at(context, i, length), 5 + i) for i in range(batch)
    ]
    for copy in element_loads(0) + first_loads:
        copy.start()

    def weight_load(ref, step):
        slot = step % 2
        return pltpu.make_async_copy(
            rows_at(ref, step, CHUNK),
            weight_rows.at[slot, :, pl.ds(0, ref.shape[1])],
            row_sem.at[slot],
        )

    out_steps, in_steps = out_ref.shape[0] // CHUNK, in_ref.shape[0] // CHUNK
    for step in range(2):
        weight_load(out_ref, step).start()
    gain_grads[...] = jnp.zeros_like(gain_grads)
    spot.greet()
    for copy in first_loads:
        copy.wait()

    def result_save(i, target):
        return pltpu.make_async_copy(result.at[i], target.at[i], save_sem.at[i])

    def half_copy(ref, i, side):
        return ref.at[pl.ds(pl.multiple_of(i * length + side * half, 16), half), pl.ds(0, width)]

    def hidden_copy(i):
        place = half_copy(hidden_grads, i, x)
        return spot.send(place, place, hidden_send.at[i], hidden_receive.at[i], CROSS)

    def element_rows(i):
        for copy in element_loads(i):
            copy.wait()

        def elementwise(step, _):
            rows = pl.ds(pl.multiple_of(step * 16, 16), 16)
            value = elements[0, rows, :]
            result[i, rows, :] = (value + elements[2, rows, :]).astype(jnp.bfloat16)
            back, gain_rows = norm_back(
                value, elements[1, rows, :], gain2_ref[...].astype(jnp.float32)
            )
            gain_grads[1:2, :] += jnp.sum(gain_rows, axis=0, keepdims=True)
            total = cots[i, rows, :].astype(jnp.float32) + back
            kept[i, rows, :] = total
            place = pl.ds(pl.multiple_of(i * length + x * half + step * 16, 16), 16)
            hidden_grads[place, :] = total.astype(jnp.bfloat16)
            return 0

        lax.fori_loop(0, half // 16, elementwise, 0)
        hidden_copy(i).start()
        result_save(i, block_out).start()
        if i + 1 < batch:
            for copy in element_loads(i + 1):
                copy.start()

    def hidden_done():
        for i in range(batch):
            hidden_copy(i).wait_send()
            place = half_copy(hidden_grads, i, 1 - x)
            spot.send(place, place, hidden_send.at[i], hidden_receive.at[i], CROSS).wait_recv()

    def context_step(step):
        weight_load(out_ref, step).wait()
        columns = slice(step * CHUNK, (step + 1) * CHUNK)
        context_grads[:, columns] = lax.dot_general(
            hidden_grads[...],
            weight_rows[step % 2, :, :width],
            TRANSPOSED_RIGHT,
            preferred_element_type=jnp.float32,
        ).astype(jnp.bfloat16)
        if step + 2 < out_steps:
            weight_load(out_ref, step + 2).start()

    def out_step(step):
        columns = slice(step * CHUNK, (step + 1) * CHUNK)
        for start in range(0, width, CHUNK):
            out_grads[columns, start : start + CHUNK] = lax.dot_general(
                context[:, columns],
                hidden_grads[:, start : start + CHUNK],
                TRANSPOSED_LEFT,
                preferred_element_type=jnp.float32,
            ).astype(jnp.bfloat16)

    tree = Collect(
        narrow,
        lambda block, side: columns_at(out_grads, block, out_width),
        out_total,
        cores,
        firsts,
        rights,
        lefts,
        tree_send,
        tree_receive,
    )

    def in_start():
        for step in range(2):
            weight_load(in_ref, step).start()

    def tree_start():
        for z in range(line):
            tree.begin(z)
        for copy in head_loads(0):
            copy.start()

    def turns():
        return [(i, shared) for i in range(batch) for shared in range(kv_heads)]

    def head_loads(index):
        i, shared = turns()[index]
        slot = index % 2
        return [
            pltpu.make_async_copy(
                projected_ref.at[i, :, pl.ds(shared * group * features, group * features)],
                queries_f.at[slot],
                head_sem.at[slot, 0],
            )
        ] + [
            pltpu.make_async_copy(
                projected_ref.at[i, :, pl.ds(base + (shared + j * kv_heads) * features, features)],
                shared_f.at[slot, j],
                head_sem.at[slot, 1 + j],
            )
            for j in range(2)
        ]

    def turn_back(grads_in):
        return grads_in * cosine_ref[...] + pltpu.roll(
            grads_in * sine_ref[...], features // 2, 1
        )

    query_gain = lambda: query_gain_ref[...].astype(jnp.float32)
    key_gain = lambda: key_gain_ref[...].astype(jnp.float32)

    def attend_pieces(index):
        i, shared = turns()[index]
        slot = index % 2
        top = i * length

        def columns_of(member):
            return pl.ds(pl.multiple_of(member * features, LANES), features)

        def prepare():
            for copy in head_loads(index):
                copy.wait()
            if index + 1 < len(turns()):
                for copy in head_loads(index + 1):
                    copy.start()
            queries[group] = turned_heads(
                shared_f[slot, 0], key_gain(), cosine_ref[...], sine_ref[...]
            ).astype(jnp.bfloat16)
            queries[group + 1] = shared_f[slot, 1].astype(jnp.bfloat16)
            sums[...] = jnp.zeros_like(sums)

            def one(member):
                queries[member] = turned_heads(
                    queries_f[slot, :, columns_of(member)],
                    query_gain(),
                    cosine_ref[...],
                    sine_ref[...],
                ).astype(jnp.bfloat16)

            for_heads(0, group, 1, one)

        def rows_block(start, stop, seen, at_once, low, high):
            count = stop - start

            def block(member):
                query = queries[pl.ds(member, at_once), start:stop, :].reshape(-1, features)
                keys, values = queries[group, :seen, :], queries[group + 1, :seen, :]
                out_grad = jnp.concatenate(
                    [
                        context_grads[
                            top + start : top + stop,
                            head_columns(shared * group + member + j, features),
                        ]
                        for j in range(at_once)
                    ],
                    axis=0,
                )
                scores = lax.dot_general(
                    keys, query, TRANSPOSED_RIGHT, preferred_element_type=jnp.float32
                )
                shares = softmax(scores * scale)
                share_grads = lax.dot_general(
                    values, out_grad, TRANSPOSED_RIGHT, preferred_element_type=jnp.float32
                )
                sums[1, :seen, :] += jnp.dot(
                    shares.astype(jnp.bfloat16), out_grad, preferred_element_type=jnp.float32
                )
                inner = jnp.sum(shares * share_grads, axis=0, keepdims=True)
                score_grads = (shares * (share_grads - inner)).astype(jnp.bfloat16)
                rows = scale * lax.dot_general(
                    score_grads, keys, TRANSPOSED_LEFT, preferred_element_type=jnp.float32
                )
                query_grads[pl.ds(member, at_once), start:stop, :] = rows.reshape(
                    at_once, count, features
                )
                sums[0, :seen, :] += jnp.dot(
                    score_grads, query, preferred_element_type=jnp.float32
                )

            for_heads(low, high, at_once, block)

        def finish_queries():
            def finish(member):
                back, gain_rows = norm_back(
                    queries_f[slot, :, columns_of(member)],
                    turn_back(query_grads[member]),
                    query_gain(),
                )
                gain_grads[2:3, :features] += jnp.sum(gain_rows, axis=0, keepdims=True)
                grads[top : top + length, head_columns(shared * group + member, features)] = (
                    back.astype(jnp.bfloat16)
                )

            for_heads(0, group, 1, finish)

        def finish_keys():
            back, gain_rows = norm_back(shared_f[slot, 0], turn_back(sums[0] * scale), key_gain())
            gain_grads[3:4, :features] += jnp.sum(gain_rows, axis=0, keepdims=True)
            at = base + shared * features
            grads[top : top + length, at : at + features] = back.astype(jnp.bfloat16)
            at += kv_heads * features
            grads[top : top + length, at : at + features] = sums[1].astype(jnp.bfloat16)

        pieces = [prepare]
        for start, stop, seen, at_once in visible_blocks(length, group):
            share = max(at_once, group // 2)
            for low in range(0, group, share):
                pieces.append(
                    functools.partial(rows_block, start, stop, seen, at_once, low, low + share)
                )
        return pieces + [finish_queries, finish_keys]

    saves = [
        pltpu.make_async_copy(rows_at(grads, i, length), grads_all.at[i], save_sem.at[batch + i])
        for i in range(batch)
    ]

    def normed_step(step):
        weight_load(in_ref, step).wait()
        normed_grads[:, step * CHUNK : (step + 1) * CHUNK] = lax.dot_general(
            grads[...],
            weight_rows[step % 2],
            TRANSPOSED_RIGHT,
            preferred_element_type=jnp.float32,
        ).astype(jnp.bfloat16)
        if step + 2 < in_steps:
            weight_load(in_ref, step + 2).start()

    def normed_copy(i):
        return spot.send(
            half_copy(normed_grads, i, 1 - x),
            normed_other.at[i],
            normed_send.at[i],
            normed_receive.at[i],
            CROSS,
        )

    def input_rows(i):
        normed_copy(i).wait()
        result_save(i, block_out).wait()

        def body(step, _):
            rows = pl.ds(pl.multiple_of(step * 16, 16), 16)
            place = pl.ds(pl.multiple_of(i * length + x * half + step * 16, 16), 16)
            total = normed_grads[place, :width].astype(jnp.float32) + normed_other[
                i, rows, :
            ].astype(jnp.float32)
            back, gain_rows = norm_back(
                tokens[i, rows, :].astype(jnp.float32), total, gain1_ref[...].astype(jnp.float32)
            )
            gain_grads[0:1, :] += jnp.sum(gain_rows, axis=0, keepdims=True)
            kept[i, rows, :] = kept[i, rows, :] + back
            return 0

        lax.fori_loop(0, half // 16, body, 0)
        add_rows(result.at[i], [kept.at[i]])
        result_save(i, input_grad).start()

    opening = [functools.partial(element_rows, i) for i in range(batch)] + [hidden_done]
    opening += [functools.partial(out_step, step) for step in range(out_steps)]
    opening += [tree_start, functools.partial(context_step, 0), tree.cross]
    opening += [functools.partial(context_step, step) for step in range(1, out_steps)]
    opening.append(in_start)
    attending = [piece for index in range(len(turns())) for piece in attend_pieces(index)]
    closing = attending + [copy.start for copy in saves]
    closing += [functools.partial(normed_step, step) for step in range(in_steps)]
    closing += [normed_copy(i).start for i in range(batch)]
    closing += [functools.partial(input_rows, i) for i in range(batch)]
    for piece in opening:
        piece()
    mingle(closing, tree.tasks())
    for i in range(batch):
        result_save(i, input_grad).wait()
    for copy in saves:
        copy.wait()


def run_backward(
    cot,
    totals,
    hidden,
    projected,
    context,
    in_full,
    out_full,
    tokens,
    gains,
    tables,
    fsdp_count,
    kv_heads,
):
    line = fsdp_count // PLANE
    batch, half, width = tokens.shape
    length = 2 * half
    features = gains[2].shape[1]
    heads = out_full.shape[0] // features
    group = heads // kv_heads
    in_width, out_depth = in_full.shape[1], out_full.shape[0]
    out_shape = (out_depth, width // fsdp_count)
    anywhere = pl.BlockSpec(memory_space=pl.ANY)
    inside = pl.BlockSpec(memory_space=pltpu.VMEM)
    shape = lambda *dims: jax.ShapeDtypeStruct(dims, jnp.bfloat16)
    vmem = lambda *dims: pltpu.VMEM(dims, jnp.bfloat16)
    wide = lambda *dims: pltpu.VMEM(dims, jnp.float32)
    sem = lambda *dims: pltpu.SemaphoreType.DMA(dims)
    rows = batch * length
    return pl.pallas_call(
        functools.partial(backward_kernel, line, heads, kv_heads),
        out_shape=(
            shape(batch, half, width),
            shape(batch, half, width),
            shape(batch, length, in_width),
            jax.ShapeDtypeStruct(out_shape, jnp.float32),
            jax.ShapeDtypeStruct((8, width), jnp.float32),
        ),
        in_specs=[anywhere] * 8 + [inside] * 6,
        out_specs=(anywhere, anywhere, anywhere, inside, inside),
        scratch_shapes=[
            wide(3, half, width),
            vmem(batch, half, width),
            vmem(batch, half, width),
            wide(batch, half, width),
            vmem(batch, half, width),
            vmem(rows, out_depth),
            vmem(rows, width),
            vmem(rows, max(out_depth, width)),
            vmem(rows, in_width),
            vmem(batch, half, width),
            vmem(2, CHUNK, max(width, in_width)),
            wide(2, length, group * features),
            wide(2, 2, length, features),
            vmem(group + 2, length, features),
            wide(group, length, features),
            wide(2, length, features),
            vmem(out_depth, width),
            *collect_scratch(line, out_shape),
            sem(5 + batch),
            sem(2),
            sem(2, 3),
            sem(2 * batch),
            sem(batch),
            sem(batch),
            sem(batch),
            sem(batch),
        ],
        compiler_params=pltpu.CompilerParams(
            collective_id=3, has_side_effects=True, vmem_limit_bytes=62 * MIB
        ),
    )(
        cot,
        totals,
        hidden,
        projected,
        context,
        in_full,
        out_full,
        tokens,
        *gains,
        *tables,
    )


def gradients_kernel(
    line,
    normed,
    grads,
    gains_ref,
    xe_ref,
    ce_ref,
    act_ref,
    dgate_ref,
    dup_ref,
    in_total,
    gains_all,
    gate_total,
    up_total,
    down_total,
    parts,
    cores,
    firsts,
    rights,
    lefts,
    tree_send,
    tree_receive,
    gain_send,
    gain_receive,
    gain_local,
    wide_rows,
    slim_rows,
    gate_sum,
    up_sum,
    down_sum,
    load_sem,
    save_sem,
):
    narrow, spot = Spot(line, False), Spot(line, True)
    experts, count, _ = xe_ref.shape
    share = wide_rows.shape[1]
    turns = count // share
    pieces = [
        (expert, kind, turn)
        for expert in range(experts)
        for kind in range(2)
        for turn in range(turns)
    ]

    def loads(index):
        expert, kind, turn = pieces[index]
        slot = index % 2
        rows = pl.ds(turn * share, share)
        slim = (dgate_ref, dup_ref) if kind == 0 else (act_ref,)
        return [
            pltpu.make_async_copy(
                (xe_ref, ce_ref)[kind].at[expert, rows], wide_rows.at[slot], load_sem.at[slot, 0]
            )
        ] + [
            pltpu.make_async_copy(
                ref.at[expert, rows], slim_rows.at[slot, i], load_sem.at[slot, 1 + i]
            )
            for i, ref in enumerate(slim)
        ]

    def saves(expert, kind):
        pairs = ((gate_sum, gate_total), (up_sum, up_total))
        if kind:
            return [pltpu.make_async_copy(down_sum, down_total.at[expert], save_sem.at[2])]
        return [
            pltpu.make_async_copy(source, target.at[expert], save_sem.at[i])
            for i, (source, target) in enumerate(pairs)
        ]

    for copy in loads(0):
        copy.start()
    spot.greet()
    gains = Spread(
        spot,
        gains_ref,
        lambda block, half: gains_all.at[block, half],
        gain_send,
        gain_receive,
        gain_local.at[0],
    )
    gains.begin()
    depth, width = in_total.shape
    tree = Collect(
        narrow,
        lambda block, half: rows_at(parts, block, depth),
        in_total,
        cores,
        firsts,
        rights,
        lefts,
        tree_send,
        tree_receive,
    )
    chunk = PLANE * depth

    def plane(step, _):
        z = lax.rem(narrow.z + 1 + step, line)
        columns = pl.ds(pl.multiple_of(z * chunk, LANES), chunk)
        for start in range(0, width, CHUNK):
            parts[pl.ds(pl.multiple_of(z * chunk, 16), chunk), start : start + CHUNK] = (
                lax.dot_general(
                    normed[:, columns],
                    grads[:, start : start + CHUNK],
                    TRANSPOSED_LEFT,
                    preferred_element_type=jnp.float32,
                ).astype(jnp.bfloat16)
            )
        tree.begin(z)
        return 0

    lax.fori_loop(0, line, plane, 0)

    def piece(index):
        expert, kind, turn = pieces[index]
        slot = index % 2
        for copy in loads(index):
            copy.wait()
        if index + 1 < len(pieces):
            for copy in loads(index + 1):
                copy.start()
        if turn == 0 and expert:
            for copy in saves(expert - 1, kind):
                copy.wait()
        size = wide_rows.shape[2] // 4

        def add(target, place, left, right):
            product = lax.dot_general(
                left, right, TRANSPOSED_LEFT, preferred_element_type=jnp.float32
            )
            if turn:
                product = target[place] + product
            target[place] = product

        def part(step, _):
            at = pl.ds(pl.multiple_of(step * size, LANES), size)
            if kind:
                add(down_sum, (slice(None), at), slim_rows[slot, 0], wide_rows[slot, :, at])
            else:
                for i, target in enumerate((gate_sum, up_sum)):
                    add(target, (at, slice(None)), wide_rows[slot, :, at], slim_rows[slot, i])
            return 0

        lax.fori_loop(0, 4, part, 0)
        if turn == turns - 1:
            for copy in saves(expert, kind):
                copy.start()

    tree.cross()
    work = tree.tasks()
    steps = list(range(1, gains.steps()))
    filler = list(range(len(pieces)))
    while work or filler:
        for _ in range(2 if len(filler) > len(work) else 1):
            if filler:
                piece(filler.pop(0))
        if work:
            work.pop(0)()
        if steps:
            gains.step(steps.pop(0))
    gains.finish()
    for copy in saves(experts - 1, 0) + saves(experts - 1, 1):
        copy.wait()


def run_gradients(normed, grads, gains, expert_rows, fsdp_count):
    line = fsdp_count // PLANE
    width = grads.shape[1]
    experts, count, depth = expert_rows[0].shape
    units = expert_rows[2].shape[2]
    share = 2 * CHUNK if count % (2 * CHUNK) == 0 else count // (2 * line)
    shape = (normed.shape[1] // fsdp_count, width)
    sends, receives = spread_count(line, True)
    inside = pl.BlockSpec(memory_space=pltpu.VMEM)
    anywhere = pl.BlockSpec(memory_space=pl.ANY)
    return pl.pallas_call(
        functools.partial(gradients_kernel, line),
        out_shape=(
            jax.ShapeDtypeStruct(shape, jnp.float32),
            jax.ShapeDtypeStruct((fsdp_count, 2, *gains.shape), jnp.float32),
            jax.ShapeDtypeStruct((experts, depth, units), jnp.float32),
            jax.ShapeDtypeStruct((experts, depth, units), jnp.float32),
            jax.ShapeDtypeStruct((experts, units, depth), jnp.float32),
        ),
        in_specs=[inside, inside] + [anywhere] * 6,
        out_specs=(inside,) + (anywhere,) * 4,
        scratch_shapes=[
            pltpu.VMEM((normed.shape[1], width), jnp.bfloat16),
            *collect_scratch(line, shape),
            pltpu.SemaphoreType.DMA((sends,)),
            pltpu.SemaphoreType.DMA((receives,)),
            pltpu.SemaphoreType.DMA((1,)),
            pltpu.VMEM((2, share, depth), jnp.bfloat16),
            pltpu.VMEM((2, 2, share, units), jnp.bfloat16),
            pltpu.VMEM((depth, units), jnp.float32),
            pltpu.VMEM((depth, units), jnp.float32),
            pltpu.VMEM((units, depth), jnp.float32),
            pltpu.SemaphoreType.DMA((2, 3)),
            pltpu.SemaphoreType.DMA((3,)),
        ],
        compiler_params=pltpu.CompilerParams(
            collective_id=4, has_side_effects=True, vmem_limit_bytes=60 * MIB
        ),
    )(normed, grads, gains, *expert_rows)


def experts_kernel(
    line,
    slots,
    own_ref,
    cot_first,
    cot_ref,
    info_ref,
    gate_ref,
    up_ref,
    down_ref,
    all_ref,
    cot_later,
    total_ref,
    xe_all,
    ce_all,
    act_all,
    dgate_all,
    dup_all,
    part,
    cores,
    seconds,
    firsts,
    ends,
    hidden_w,
    down_w,
    x_rows,
    c_rows,
    xe,
    ce,
    acts,
    dgates,
    dups,
    hidden_grads,
    picks,
    weigh,
    rows,
    stage,
    inbox,
    outbox,
    summed,
    rows_send,
    rows_receive,
    rows_late_send,
    rows_late_receive,
    rows_local,
    cot_send,
    cot_receive,
    cot_late_send,
    cot_late_receive,
    cot_local,
    load_sem,
    save_sem,
    stage_sem,
    inbox_sem,
    outbox_sem,
    total_sem,
    weight_sem,
    core_receive,
    second_receive,
    first_receive,
    end_receive,
):
    spot = Spot(line, True)
    z, core = spot.z, spot.core
    cot_semaphores = (cot_send, cot_receive, cot_late_send, cot_late_receive, cot_local)
    tree_semaphores = (rows_send, rows_receive, rows_late_send, rows_late_receive, rows_local)
    batch, half, width = own_ref.shape
    length = 2 * half
    units = down_ref.shape[1]
    groups = batch * line
    weights = [
        pltpu.make_async_copy(source, target, weight_sem.at[i])
        for i, (source, target) in enumerate(
            [(down_ref, down_w)]
            + [(gate_ref.at[e], hidden_w.at[e, :, pl.ds(0, units)]) for e in range(2)]
            + [(up_ref.at[e], hidden_w.at[e, :, pl.ds(units, units)]) for e in range(2)]
        )
    ]
    for copy in weights:
        copy.start()
    rows[...] = jnp.zeros_like(rows)
    spot.greet()

    def half_of(ref, index):
        return rows_at(ref, index, half)

    trees = []
    for i in range(batch):
        place = lambda block, start, size, i=i: all_ref.at[
            i, block, pl.ds(pl.multiple_of(start, 16), size)
        ]
        trees.append(rows_spread(spot, own_ref.at[i], place, half, tree_semaphores, i))
    for i in range(1, batch):
        place = lambda block, start, size, i=i: cot_later.at[
            i - 1, block, pl.ds(pl.multiple_of(start, 16), size)
        ]
        trees[i] += rows_spread(spot, cot_ref.at[i], place, half, cot_semaphores, i - 1)
    run_trees(trees[0])
    for tree in sum(trees[1:], []):
        tree.begin()
    for copy in weights:
        copy.wait()

    plane_of = functools.partial(plane_in_turn, line)

    def load_group(group, member, start):
        at = lax.div(group, line)
        sequence = plane_of(group) * PLANE + member
        slot = member % 2
        def copy(i, source, target):
            return pltpu.make_async_copy(source, target.at[slot], load_sem.at[i, slot])

        own = copy(0, all_ref.at[at, sequence], x_rows)
        if start:
            own.start()
            later = cot_later.at[jnp.maximum(at - 1, 0), sequence]
            when(at == 0, lambda: copy(1, cot_first.at[sequence], c_rows).start())
            when(at > 0, lambda: copy(1, later, c_rows).start())
        else:
            own.wait()
            copy(1, cot_first.at[sequence], c_rows).wait()

    def saves(group):
        to = lambda ref, expert: rows_at(ref.at[expert], group, PLANE * slots)
        pairs = ((xe, xe_all), (ce, ce_all), (acts, act_all), (dgates, dgate_all), (dups, dup_all))
        return [
            pltpu.make_async_copy(source.at[expert], to(target, expert), save_sem.at[2 * i + expert])
            for i, (source, target) in enumerate(pairs)
            for expert in range(2)
        ]

    def staged(unit, y, mine):
        slot = y * 2 + mine
        if mine:
            return pltpu.make_async_copy(stage.at[slot], part.at[unit, y], stage_sem.at[slot])
        return spot.send(
            stage.at[slot], cores.at[unit, y], stage_sem.at[slot], core_receive.at[unit, y], CORE
        )

    def combine(unit, y):
        for mine in range(2):
            member = y * 2 + (core if mine else 1 - core)
            for start in range(0, width, CHUNK):
                stage[y * 2 + mine, :, start : start + CHUNK] = lax.dot_general(
                    picks[member],
                    rows[member, :, start : start + CHUNK],
                    TRANSPOSED_LEFT,
                    preferred_element_type=jnp.float32,
                ).astype(jnp.bfloat16)
            staged(unit, y, mine).start()

    def pick(group, member):
        slot = member % 2
        load_group(group, member, False)
        if member + 1 < PLANE:
            load_group(group, member + 1, True)
        sequence = plane_of(group) * PLANE + member
        info = info_ref[lax.div(group, line) * line * PLANE + sequence]
        places = lax.broadcasted_iota(jnp.int32, (2 * LANES, length), 0)
        lower = places < LANES
        ranks = jnp.where(lower, info[0:1], info[1:2] + float(LANES)).astype(jnp.int32)
        some = jnp.where(lower, info[0:1], info[1:2]) >= 0.0
        hot = jnp.logical_and(ranks == places, some)
        chosen = hot.astype(jnp.float32).astype(jnp.bfloat16)
        picks[member] = chosen
        shares = jnp.where(hot, jnp.where(lower, info[2:3], info[3:4]), 0.0)
        column = jnp.sum(shares, axis=1, keepdims=True)
        here = pl.ds(member * slots, slots)
        for expert in range(2):
            weigh[expert, here, :] = jnp.broadcast_to(
                column[expert * LANES : expert * LANES + slots], (slots, LANES)
            )
        for source, target in ((x_rows, xe), (c_rows, ce)):
            for start in range(0, width, CHUNK):
                selected = jnp.dot(
                    chosen,
                    source[slot, :, start : start + CHUNK],
                    preferred_element_type=jnp.float32,
                ).astype(jnp.bfloat16)
                for expert in range(2):
                    target[expert, here, start : start + CHUNK] = selected[
                        expert * LANES : expert * LANES + slots
                    ]

    def keep(expert, product, start):
        at = pl.ds(expert * LANES, slots)
        for one in range(PLANE):
            rows[one, at, start : start + CHUNK] = product[one * slots : (one + 1) * slots].astype(
                jnp.bfloat16
            )

    def forward(expert):
        hidden = jnp.dot(xe[expert], hidden_w[expert], preferred_element_type=jnp.float32)
        gate, up = hidden[:, :units], hidden[:, units:]
        sigmoid = jax.nn.sigmoid(gate)
        silu = gate * sigmoid
        scale = weigh[expert, :, 0:1]
        acts[expert] = (silu * up * scale).astype(jnp.bfloat16)
        act_grads = scale * lax.dot_general(
            ce[expert], down_w[expert], TRANSPOSED_RIGHT, preferred_element_type=jnp.float32
        )
        gate_grads = (act_grads * up * (sigmoid * (1.0 + gate * (1.0 - sigmoid)))).astype(
            jnp.bfloat16
        )
        up_grads = (act_grads * silu).astype(jnp.bfloat16)
        dgates[expert] = gate_grads
        dups[expert] = up_grads
        hidden_grads[expert, :, :units] = gate_grads
        hidden_grads[expert, :, units:] = up_grads
        for start in range(0, width, CHUNK):
            keep(
                expert,
                jnp.dot(
                    acts[expert],
                    down_w[expert, :, start : start + CHUNK],
                    preferred_element_type=jnp.float32,
                ),
                start,
            )

    def backward(expert):
        for start in range(0, width, CHUNK):
            keep(
                expert,
                lax.dot_general(
                    hidden_grads[expert],
                    hidden_w[expert, start : start + CHUNK, :],
                    TRANSPOSED_RIGHT,
                    preferred_element_type=jnp.float32,
                ),
                start,
            )

    units_all = 2 * groups

    def inside(unit):
        return jnp.logical_and(unit >= 0, unit < units_all)

    def ready(unit):
        @pl.when(inside(unit))
        def _():
            for y in range(2):
                staged(unit, y, 1).wait()
                staged(unit, y, 0).wait_send()
                place, semaphore = cores.at[unit, y], core_receive.at[unit, y]
                spot.send(place, place, outbox_sem.at[0], semaphore, CORE).wait_recv()

    def done(unit, tensor, into):
        into(summed)
        copy = pltpu.make_async_copy(
            summed, total_ref.at[lax.div(unit, 2 * line), tensor], total_sem.at[0]
        )
        copy.start()
        copy.wait()

    sums = Sums(
        spot,
        lambda unit, y: part.at[unit, y],
        lambda unit, y: cores.at[unit, y],
        (seconds, firsts, ends),
        inbox,
        outbox,
        (inbox_sem, outbox_sem, second_receive, first_receive, end_receive),
        lambda unit: plane_of(lax.div(jnp.maximum(unit, 0), 2)),
        inside,
        ready,
        done,
        2,
    )

    def tree_turn(half_step, last):
        for i in range(1, batch):
            turn = half_step - (i - 1) * 2 * line
            if last:
                when(turn == 2 * line - 1, lambda: [tree.finish() for tree in trees[i]])
            else:
                inner = jnp.logical_and(turn >= 0, turn < 2 * line - 1)
                when(inner, lambda: [tree.step(turn + 1) for tree in trees[i]])

    def begin_pick(group):
        load_group(group, 0, True)

    begin_pick(0)
    for member in range(PLANE):
        pick(0, member)

    def step_body(step, _):
        busy = step < groups
        more = step + 1 < groups
        for parity in range(2):
            half_step = step * 2 + parity
            tree_turn(half_step, False)
            sums.retire(half_step, parity)
            tasks = sums.tasks(half_step, parity)
            pieces = []
            for expert in range(2):
                pieces.append(functools.partial((forward, backward)[parity], expert))
            if parity == 0:
                pieces.append(lambda: [copy.start() for copy in saves(step)])
            for y in range(2):
                pieces.append(functools.partial(combine, half_step, y))
            pieces = [functools.partial(when, busy, piece) for piece in pieces]
            if parity == 1:

                def prepare():
                    for copy in saves(step):
                        copy.wait()
                    begin_pick(step + 1)

                tree_end = functools.partial(tree_turn, half_step, True)
                pieces += [tree_end, functools.partial(when, more, prepare)]
                for member in range(PLANE):
                    pieces.append(
                        functools.partial(when, more, functools.partial(pick, step + 1, member))
                    )
            sums.weave(tasks, pieces)
        return 0

    half_steps = sums.half_steps(units_all)
    lax.fori_loop(0, -(-half_steps // 2), step_body, 0)
    end = -(-half_steps // 2) * 2
    for parity in range(2):
        sums.retire(jnp.int32(end + parity), parity)
    for copy in saves(groups - 1):
        copy.wait()


def run_experts(rows, cot_first, cot, info, w_gate, w_up, w_down, capacity, fsdp_count):
    line = fsdp_count // PLANE
    batch, half, width = rows.shape
    length = 2 * half
    units = w_down.shape[1]
    slots = -(-capacity // 16) * 16
    groups = batch * line
    count = groups * PLANE * slots
    taken = PLANE * slots
    shape = lambda *dims: jax.ShapeDtypeStruct(dims, jnp.bfloat16)
    block = (half, width)
    anywhere = pl.BlockSpec(memory_space=pl.ANY)
    vmem = lambda *dims: pltpu.VMEM(dims, jnp.bfloat16)
    sem = lambda *dims: pltpu.SemaphoreType.DMA(dims)
    return pl.pallas_call(
        functools.partial(experts_kernel, line, slots),
        out_shape=(
            shape(batch, fsdp_count, length, width),
            shape(max(batch - 1, 1), fsdp_count, length, width),
            jax.ShapeDtypeStruct((batch, 2, *block), jnp.float32),
            shape(2, count, width),
            shape(2, count, width),
            shape(2, count, units),
            shape(2, count, units),
            shape(2, count, units),
            shape(2 * groups, 2, length, width),
            shape(2 * groups, 2, length, width),
            shape(2 * groups, 2, *block),
            shape(2 * groups, *block),
            shape(2 * groups, 2, *block),
        ),
        in_specs=[
            anywhere,
            anywhere,
            anywhere,
            pl.BlockSpec(memory_space=pltpu.VMEM),
            anywhere,
            anywhere,
            anywhere,
        ],
        out_specs=(anywhere,) * 13,
        scratch_shapes=[
            vmem(2, width, 2 * units),
            vmem(2, units, width),
            vmem(2, length, width),
            vmem(2, length, width),
            vmem(2, taken, width),
            vmem(2, taken, width),
            vmem(2, taken, units),
            vmem(2, taken, units),
            vmem(2, taken, units),
            vmem(2, taken, 2 * units),
            vmem(PLANE, 2 * LANES, length),
            pltpu.VMEM((2, taken, LANES), jnp.float32),
            vmem(PLANE, 2 * LANES, width),
            vmem(PLANE, length, width),
            vmem(12, *block),
            vmem(10, *block),
            pltpu.VMEM(block, jnp.float32),
            *rows_semaphores(batch, line),
            *rows_semaphores(max(batch - 1, 1), line),
            sem(2, 2),
            sem(10),
            sem(PLANE),
            sem(12),
            sem(10),
            sem(1),
            sem(5),
            sem(2 * groups, 2),
            sem(2 * groups, 2),
            sem(2 * groups),
            sem(2 * groups, 2),
        ],
        compiler_params=pltpu.CompilerParams(
            collective_id=2, has_side_effects=True, vmem_limit_bytes=60 * MIB
        ),
    )(rows, cot_first, cot, info, w_gate, w_up, w_down)[2:8]


def packed_picks(routes, gates):
    length = routes.shape[2]
    packed = jnp.concatenate([routes[:, 0].astype(jnp.float32), gates[:, 0]], axis=-1)
    packed = jnp.swapaxes(packed, 1, 2).reshape(-1, length)
    return jnp.pad(packed, ((0, 0), (0, -length % LANES)))


def slot_info(packed, batch, top, length, local_experts):
    fsdp_count = packed.shape[0]
    packed = packed[..., :length].reshape(fsdp_count, batch, 1, 2 * top, length)
    packed = jnp.swapaxes(packed, 0, 1)
    experts = lax.axis_index(FSDP) * local_experts + jnp.arange(local_experts, dtype=jnp.int32)
    same = packed[..., :top, :].astype(jnp.int32) == experts[:, None, None]
    hot = jnp.any(same, axis=3)
    shares = jnp.sum(jnp.where(same, packed[..., top:, :], 0.0), axis=3)
    position = jnp.arange(length)
    upper = (position[:, None] < position[None, :]).astype(jnp.bfloat16)
    rank = jnp.dot(
        hot.astype(jnp.bfloat16).reshape(-1, length), upper, preferred_element_type=jnp.float32
    )
    rank = jnp.where(hot, rank.reshape(hot.shape), -1.0)
    return jnp.concatenate([rank, shares], axis=2).reshape(-1, 2 * local_experts, length)


def gathered_layer(
    tokens,
    cotangent,
    norm1_gain,
    w_query,
    key_projection_weight,
    value_projection_weight,
    query_gain,
    key_gain,
    w_out,
    norm2_gain,
    w_gate,
    w_up,
    w_down,
    routes,
    gates,
):
    batch_count = tokens.shape[0]
    model_width = tokens.shape[3]
    sequence_length = routes.shape[2]
    half_length = tokens.shape[2]
    top_count = routes.shape[3]
    head_features = query_gain.shape[0]
    local_experts = w_gate.shape[0]
    fsdp_count = lax.axis_size(FSDP)
    all_experts = local_experts * fsdp_count
    capacity = 7 * top_count * sequence_length // (6 * all_experts)
    query_width = w_query.shape[1]
    kv_width = key_projection_weight.shape[1]
    kv_heads = kv_width // head_features
    cosine_table, sine_values = rotary_tables(sequence_length, head_features)
    weight_in = jnp.concatenate([w_query, key_projection_weight, value_projection_weight], axis=1)
    half_signs = jnp.where(jnp.arange(head_features) < head_features // 2, -1.0, 1.0)
    tables = (cosine_table[:, 0], sine_values[:, 0] * half_signs)
    gains = [gain[None, :] for gain in (norm1_gain, norm2_gain, query_gain, key_gain)]
    cot_first, in_full, out_full, picks, normed, projected, contexts, hidden, second = run_forward(
        tokens[:, 0],
        cotangent[:, 0],
        weight_in,
        w_out,
        packed_picks(routes, gates),
        gains,
        tables,
        fsdp_count,
        kv_heads,
    )
    info = slot_info(picks, batch_count, top_count, sequence_length, local_experts)
    totals, *expert_rows = run_experts(
        second, cot_first, cotangent[:, 0], info, w_gate, w_up, w_down, capacity, fsdp_count
    )
    block_out, input_grad, projected_grads, out_sum, gain_grads = run_backward(
        cotangent[:, 0],
        totals,
        hidden,
        projected,
        contexts,
        in_full,
        out_full,
        tokens[:, 0],
        gains,
        tables,
        fsdp_count,
        kv_heads,
    )
    rows = batch_count * sequence_length
    in_sum, gains_all, *expert_grads = run_gradients(
        normed.reshape(rows, -1),
        projected_grads.reshape(rows, -1),
        gain_grads,
        expert_rows,
        fsdp_count,
    )
    gains_sum = jnp.sum(gains_all, axis=(0, 1))
    return (
        block_out[:, None],
        input_grad[:, None],
        gains_sum[0],
        in_sum[:, :query_width],
        in_sum[:, query_width : query_width + kv_width],
        in_sum[:, query_width + kv_width :],
        gains_sum[2, :head_features],
        gains_sum[3, :head_features],
        out_sum,
        gains_sum[1],
        *expert_grads,
    )


def shards(*arrays):
    tokens, routes, w_gate = arrays[0], arrays[13], arrays[10]
    fsdp_count = lax.axis_size(FSDP)
    gathered = fsdp_count * routes.shape[2] * tokens.shape[3] * 2
    fits = gathered <= 24 * MIB and fsdp_count % PLANE == 0 and lax.axis_size(TP) == 2
    if fits and w_gate.shape[0] == 2:
        return gathered_layer(*arrays)
    return exchanged_layer(*arrays)


def solution(mesh):
    in_specs = (
        P(None, "fsdp", "tp", None),
        P(None, "fsdp", "tp", None),
        P(),
        P("fsdp", "tp"),
        P("fsdp", "tp"),
        P("fsdp", "tp"),
        P(),
        P(),
        P("tp", "fsdp"),
        P(),
        P("fsdp", None, "tp"),
        P("fsdp", None, "tp"),
        P("fsdp", "tp", None),
        P(None, "fsdp", None, None),
        P(None, "fsdp", None, None),
    )
    out_specs = (
        P(None, "fsdp", "tp", None),
        P(None, "fsdp", "tp", None),
        P(),
        P("fsdp", "tp"),
        P("fsdp", "tp"),
        P("fsdp", "tp"),
        P(),
        P(),
        P("tp", "fsdp"),
        P(),
        P("fsdp", None, "tp"),
        P("fsdp", None, "tp"),
        P("fsdp", "tp", None),
    )
    return jax.shard_map(shards, mesh=mesh, in_specs=in_specs, out_specs=out_specs, check_vma=False)
```

profile of v0, /device:TPU:26, one launch (start us, length us, event | category | flops | bytes accessed | tf_op | source)
XLA Modules:
  0.0 1038.0 jit_solution(15531798442014545013)
XLA Ops:
  0.7 1.3 broadcast_in_dim.49.gain1_ref
  2.0 1.3 broadcast_in_dim.50.gain2_ref
  3.3 0.7 fusion.7
  4.0 0.7 pad_maximum_fusion.3
  4.8 0.6 pad.4.picks_ref
  5.4 0.6 fusion.4
  5.9 0.8 pad_maximum_fusion.2
  6.8 2.0 pad_maximum_fusion.in_ref
  8.8 205.3 %shard_map.246 = (bf16[16,288,2048]{2,1,0:T(8,128)(2,1)}, bf16[2048,2560]{1,0:T(8,128)(2,1)}, bf16[2048,2048]{1,0:T(8,128)(2,1)}, f32[16,32,384]{2,1,0:T(8,128)}...) custom-call(bf16[2,144,2048]{2,1,0:T(8,128)(2,1)} %bitcast.49, ...), custom_call_target="tpu_custom_call" | custom-call | tf_op jit(solution)/shard_map/pallas_call | solution.py:1048
  214.1 1.2 fusion.3
  215.3 0.3 fusion
  215.6 0.3 compare_reduce_fusion
  216.0 0.2 convolution_select_fusion
  216.2 0.8 copy.40
  216.9 524.3 %shard_map.247 = (bf16[2,16,288,2048]{3,2,1,0:T(8,128)(2,1)}, bf16[1,16,288,2048]{3,2,1,0:T(8,128)(2,1)}, f32[2,2,144,2048]{3,2,1,0:T(8,128)}, bf16[2,3072,2048]...) custom-call(bf16[2,144,2048]{2,1,0:T(8,128)(2,1)} %get-tuple-element, ...), custom_call_target="tpu_custom_call" | custom-call | tf_op jit(solution)/shard_map/pallas_call | solution.py:2465
  741.2 156.6 %shard_map.248 = (bf16[2,144,2048]{2,1,0:T(8,128)(2,1)}, bf16[2,144,2048]{2,1,0:T(8,128)(2,1)}, bf16[2,288,2560]{2,1,0:T(8,128)(2,1)}, f32[2048,128]{1,0:T(8,128)}, f32[8,2048]{1,0:T(8,128)}) custom-call(bf16[2,144,2048]{2,1,0:T(8,128)(2,1)} %bitcast.44, f32[2,2,144,2048]{3,2,1,0:T(8,128)} %get-tuple-element.41.totals_ref, ...), custom_call_target="tpu_custom_call" | custom-call | tf_op jit(solution)/shard_map/pallas_call | solution.py:1863
  897.8 118.6 %shard_map.249 = (f32[128,2560]{1,0:T(8,128)}, f32[16,2,8,2048]{3,2,1,0:T(8,128)}, f32[2,2048,384]{2,1,0:T(8,128)}, f32[2,2048,384]{2,1,0:T(8,128)}, f32[2,384,2048]{2,1,0:T(8,128)}) custom-call(bf16[576,2048]{1,0:T(8,128)(2,1)} %bitcast.52, bf16[576,2560]{1,0:T(8,128)(2,1)} %bitcast.51, f32[8,2048]{1,0:T(8,128)} %get-tuple-element.51.gains_ref, ...), custom_call_target="tpu_custom_call" | custom-call | tf_op jit(solution)/shard_map/pallas_call | solution.py:2093
  1016.4 0.0 copy-start.2
  1016.5 1.9 reduce_sum.19
  1018.3 0.5 slice_bitcast_fusion.1
  1018.8 0.6 fusion.9
  1019.4 1.8 fusion.8
  1021.3 2.5 slice.34
  1023.8 1.0 copy.58
  1024.8 1.0 copy.59
  1025.8 1.0 copy.60
  1026.8 3.2 copy.61
  1030.0 0.3 slice-done.3
  1030.3 3.2 copy.62
  1033.5 0.1 slice-done
  1033.6 1.3 slice-done.1
  1034.9 2.7 copy.63
  (19 shorter events, 0.1 us)
Async XLA Ops:
  1016.4 7.4 copy-start.2
  1016.4 8.4 copy-start.1
  1016.4 9.4 copy-start.3
  1019.4 7.3 copy-start
  1024.8 5.2 slice-start.2
  1026.8 3.5 slice-start.3
  1026.8 6.8 slice-start
  1030.3 4.5 slice-start.1
where the time goes:
time: 1050 us; the launch traced here: 1040 us
  Pallas kernels  1000 us (95%)
  local copies, waits for them, and re-layouts  23.2 us (2%)
    pallas_call x1, Pallas kernels, run_experts(): pl.pallas_call(functools.partial(experts_kernel, line, slots), out_shape=...  524 us
    pallas_call x1, Pallas kernels, run_forward(): pl.pallas_call(functools.partial(forward_kernel, line, heads, kv_heads),...  205 us
    pallas_call x1, Pallas kernels, run_backward(): pl.pallas_call(functools.partial(backward_kernel, line, heads, kv_heads),...  157 us
    pallas_call x1, Pallas kernels, run_gradients(): pl.pallas_call(functools.partial(gradients_kernel, line), out_shape=(jax....  119 us

commit v1 on v0

--- a/solution.py
+++ b/solution.py
@@ -1197,8 +1197,25 @@
 
 
 class Sums:
-    def __init__(self, spot, parts, cores, places, inbox, outbox, semaphores, plane, inside, ready, done, turns):
+    def __init__(
+        self, spot, half, parts, cores, places, inbox, outbox, semaphores, late, plane, inside, ready, done, turns
+    ):
         self.spot = spot
+        self.half = half
+        (
+            self.late_ends,
+            self.late_seconds,
+            self.late_firsts,
+            self.late_inbox,
+            self.late_outbox,
+            self.late_sums,
+            self.late_inbox_sem,
+            self.late_outbox_sem,
+            self.late_sums_sem,
+            self.late_end_receive,
+            self.late_second_receive,
+            self.late_first_receive,
+        ) = late
         self.parts = parts
         self.cores = cores
         self.seconds, self.firsts, self.ends = places
@@ -1264,8 +1281,8 @@
 
     def sources(self, unit, first, second):
         y, x = self.spot.side(self.spot.core, first, second)
-        half = self.inbox.shape[1]
-        return [rows_at(self.parts(unit, y), x, half), rows_at(self.cores(unit, y), x, half)]
+        rows = pl.ds(pl.multiple_of(x * self.half, 16), self.inbox.shape[1])
+        return [self.parts(unit, y).at[rows], self.cores(unit, y).at[rows]]
 
     def summands(self, unit):
         return self.sources(unit, 0, 0) + [self.seconds.at[unit, 0], self.firsts.at[unit]]
@@ -1342,7 +1359,7 @@
                                 lambda: self.add(target, base, numbers + [4 + kind]),
                             )
 
-                    self.done(unit, turn, into)
+                    self.done(unit, turn, 0, into)
 
                 when(last, finish)
 
@@ -1359,12 +1376,14 @@
         )
         when(self.inside(before - 2), lambda: self.first_send(before - 2, then).wait_send())
         for delay in range(self.spot.line):
-            if self.inside(before - 3 - delay) is False:
-                continue
             unit, right, left, _ = self.end_roles(before, delay)
             turn = (parity - 3 - delay) % self.turns
             when(right, lambda: self.end_send(unit, turn, RIGHT).wait_send())
             when(left, lambda: self.end_send(unit, turn, LEFT).wait_send())
+            unit, right, left, _ = self.end_roles(before + 2, delay)
+            turn = (parity - 1 - delay) % self.turns
+            when(right, lambda: self.late_send(unit, turn, RIGHT).wait_send())
+            when(left, lambda: self.late_send(unit, turn, LEFT).wait_send())
 
     def simple_task(self, valid, ready, inputs, slot, send, free=lambda: None):
         def fetch(base):
@@ -1397,10 +1416,167 @@
             self.second_task(one, now, 0, lambda: None),
             self.first_task(two, then),
         ]
-        for delay in range(self.spot.line):
-            if self.inside(half_step - 3 - delay) is not False:
-                tasks.append(self.end_task(half_step, delay, parity))
-        return tasks
+        line = self.spot.line
+        tasks += [self.end_task(half_step, delay, parity) for delay in range(line)]
+        others = [self.late_task(half_step, delay, parity) for delay in range(line)]
+        others += [self.plane_task(half_step, stage) for stage in range(2)]
+        woven = []
+        for index, task in enumerate(tasks):
+            woven += [task] + others[index : index + 1]
+        return woven + others[len(tasks) :]
+
+    def late_rows(self, index):
+        return pl.ds(pl.multiple_of(index * self.late_inbox.shape[1] // 4, 16), self.late_inbox.shape[1] // 4)
+
+    def late_send(self, unit, turn, kind):
+        slot = turn * 2 + kind
+        return self.spot.send(
+            self.late_outbox.at[slot],
+            self.late_ends.at[unit, kind],
+            self.late_outbox_sem.at[slot],
+            self.late_end_receive.at[unit, kind],
+            kind,
+        )
+
+    def late_place(self, turn, first, second):
+        y, x = self.spot.side(self.spot.core, first, second)
+        return self.late_sums.at[turn, self.late_rows(y * 2 + x)]
+
+    def late_second(self, unit, turn, first):
+        return self.spot.send(
+            self.late_place(turn, first, 1),
+            self.late_seconds.at[unit, first],
+            self.late_sums_sem.at[turn * 3 + first],
+            self.late_second_receive.at[unit, first],
+            SECOND,
+        )
+
+    def late_first(self, unit, turn):
+        return self.spot.send(
+            self.late_place(turn, 1, 0),
+            self.late_firsts.at[unit],
+            self.late_sums_sem.at[turn * 3 + 2],
+            self.late_first_receive.at[unit],
+            FIRST,
+        )
+
+    def late_load(self, source, target, index):
+        return pltpu.make_async_copy(source, target, self.late_inbox_sem.at[index])
+
+    def late_loads(self, unit):
+        copies = []
+        size = self.late_inbox.shape[1] // 4
+        for y in range(2):
+            for x in range(2):
+                rows = pl.ds(x * self.half + self.half - size, size)
+                for i, ref in enumerate((self.parts(unit, y), self.cores(unit, y))):
+                    place = self.late_inbox.at[i, pl.ds((y * 2 + x) * size, size)]
+                    copies.append(self.late_load(ref.at[rows], place, i * 4 + y * 2 + x))
+        return copies
+
+    def late_task(self, half_step, delay, parity):
+        z, line = self.spot.z, self.spot.line
+        turn = (parity - 1 - delay) % self.turns
+        unit, right, left, last = self.end_roles(half_step + 2, delay)
+        some = jnp.logical_or(right, jnp.logical_or(left, last))
+        from_left = jnp.logical_and(jnp.logical_or(right, last), z > 0)
+        from_right = jnp.logical_and(jnp.logical_or(left, last), z + 1 < line)
+        present = ((RIGHT, from_left), (LEFT, from_right))
+        both = jnp.logical_and(from_left, from_right)
+
+        def behind(kind):
+            return self.late_load(self.late_ends.at[unit, kind], self.late_inbox.at[2 + kind], 8 + kind)
+
+        def fetch(base):
+            def action():
+                for copy in self.late_loads(unit):
+                    copy.start()
+                for kind, there in present:
+
+                    def arrive():
+                        self.received(self.late_ends.at[unit, kind], self.late_end_receive.at[unit, kind])
+                        behind(kind).start()
+
+                    when(there, arrive)
+
+            when(some, action)
+
+        def add(base):
+            def total(target, kinds):
+                add_rows(target, [self.late_inbox.at[i] for i in [0, 1] + [2 + kind for kind in kinds]])
+
+            def action():
+                for copy in self.late_loads(unit):
+                    copy.wait()
+                for kind, there in present:
+                    when(there, lambda: behind(kind).wait())
+                for kind, chosen, there in ((RIGHT, right, from_left), (LEFT, left, from_right)):
+
+                    def onward():
+                        target = self.late_outbox.at[turn * 2 + kind]
+                        when(there, lambda: total(target, [kind]))
+                        when(jnp.logical_not(there), lambda: total(target, []))
+                        self.late_send(unit, turn, kind).start()
+
+                    when(chosen, onward)
+
+                def in_plane():
+                    target = self.late_sums.at[turn]
+                    when(both, lambda: total(target, [RIGHT, LEFT]))
+                    for kind, there in present:
+                        when(
+                            jnp.logical_and(there, jnp.logical_not(both)),
+                            lambda: total(target, [kind]),
+                        )
+                    for first in (1, 0):
+                        self.late_second(unit, turn, first).start()
+
+                when(last, in_plane)
+
+            when(some, action)
+
+        return fetch, add
+
+    def plane_task(self, half_step, stage):
+        z, line = self.spot.z, self.spot.line
+        unit = half_step - 2 - stage - jnp.maximum(z, line - 1 - z)
+        turn = lax.rem(jnp.maximum(unit, 0), self.turns)
+        valid = jnp.logical_and(self.inside(unit), self.plane(unit) == z)
+        size = self.late_inbox.shape[1] // 4
+        place = lambda i: self.late_inbox.at[i, pl.ds(0, size)]
+        second = self.late_load(self.late_seconds.at[unit, 1 - stage], place(0), 0)
+        first = lambda: self.late_load(self.late_firsts.at[unit], place(1), 4)
+
+        def fetch(base):
+            def action():
+                self.received(
+                    self.late_seconds.at[unit, 1 - stage], self.late_second_receive.at[unit, 1 - stage]
+                )
+                second.start()
+                if stage:
+                    self.received(self.late_firsts.at[unit], self.late_first_receive.at[unit])
+                    first().start()
+
+            when(valid, action)
+
+        def add(base):
+            def action():
+                second.wait()
+                if stage:
+                    first().wait()
+                    sources = [self.late_place(turn, 0, 0), place(0), place(1)]
+                    self.done(unit, lax.rem(unit, 2), 1, lambda target: add_rows(target, sources))
+                    for i in range(2):
+                        self.late_second(unit, turn, i).wait_send()
+                    self.late_first(unit, turn).wait_send()
+                else:
+                    target = self.late_place(turn, 1, 0)
+                    add_rows(target, [target, place(0)])
+                    self.late_first(unit, turn).start()
+
+            when(valid, action)
+
+        return fetch, add
 
     def second_task(self, unit, turn, first, ready):
         return self.simple_task(
@@ -2144,6 +2320,9 @@
     seconds,
     firsts,
     ends,
+    late_ends,
+    late_seconds,
+    late_firsts,
     hidden_w,
     down_w,
     x_rows,
@@ -2182,7 +2361,9 @@
     second_receive,
     first_receive,
     end_receive,
+    *late_scratch,
 ):
+    late_refs = (late_ends, late_seconds, late_firsts, *late_scratch)
     spot = Spot(line, True)
     z, core = spot.z, spot.core
     cot_semaphores = (cot_send, cot_receive, cot_late_send, cot_late_receive, cot_local)
@@ -2368,22 +2549,28 @@
                 place, semaphore = cores.at[unit, y], core_receive.at[unit, y]
                 spot.send(place, place, outbox_sem.at[0], semaphore, CORE).wait_recv()
 
-    def done(unit, tensor, into):
-        into(summed)
+    late = late_rows(half)
+
+    def done(unit, tensor, part_of, into):
+        rows = (pl.ds(0, half - late), pl.ds(half - late, late))[part_of]
+        place = summed.at[rows]
+        into(place)
         copy = pltpu.make_async_copy(
-            summed, total_ref.at[lax.div(unit, 2 * line), tensor], total_sem.at[0]
+            place, total_ref.at[lax.div(unit, 2 * line), tensor, rows], total_sem.at[0]
         )
         copy.start()
         copy.wait()
 
     sums = Sums(
         spot,
+        half,
         lambda unit, y: part.at[unit, y],
         lambda unit, y: cores.at[unit, y],
         (seconds, firsts, ends),
         inbox,
         outbox,
         (inbox_sem, outbox_sem, second_receive, first_receive, end_receive),
+        late_refs,
         lambda unit: plane_of(lax.div(jnp.maximum(unit, 0), 2)),
         inside,
         ready,
@@ -2459,6 +2646,8 @@
     taken = PLANE * slots
     shape = lambda *dims: jax.ShapeDtypeStruct(dims, jnp.bfloat16)
     block = (half, width)
+    late = late_rows(half)
+    early = half - late
     anywhere = pl.BlockSpec(memory_space=pl.ANY)
     vmem = lambda *dims: pltpu.VMEM(dims, jnp.bfloat16)
     sem = lambda *dims: pltpu.SemaphoreType.DMA(dims)
@@ -2475,9 +2664,12 @@
             shape(2, count, units),
             shape(2 * groups, 2, length, width),
             shape(2 * groups, 2, length, width),
-            shape(2 * groups, 2, *block),
-            shape(2 * groups, *block),
-            shape(2 * groups, 2, *block),
+            shape(2 * groups, 2, early, width),
+            shape(2 * groups, early, width),
+            shape(2 * groups, 2, early, width),
+            shape(2 * groups, 2, 4 * late, width),
+            shape(2 * groups, 2, late, width),
+            shape(2 * groups, late, width),
         ),
         in_specs=[
             anywhere,
@@ -2488,7 +2680,7 @@
             anywhere,
             anywhere,
         ],
-        out_specs=(anywhere,) * 13,
+        out_specs=(anywhere,) * 16,
         scratch_shapes=[
             vmem(2, width, 2 * units),
             vmem(2, units, width),
@@ -2504,8 +2696,8 @@
             pltpu.VMEM((2, taken, LANES), jnp.float32),
             vmem(PLANE, 2 * LANES, width),
             vmem(PLANE, length, width),
-            vmem(12, *block),
-            vmem(10, *block),
+            vmem(12, early, width),
+            vmem(10, early, width),
             pltpu.VMEM(block, jnp.float32),
             *rows_semaphores(batch, line),
             *rows_semaphores(max(batch - 1, 1), line),
@@ -2520,6 +2712,15 @@
             sem(2 * groups, 2),
             sem(2 * groups),
             sem(2 * groups, 2),
+            vmem(4, 4 * late, width),
+            vmem(4, 4 * late, width),
+            vmem(2, 4 * late, width),
+            sem(10),
+            sem(4),
+            sem(6),
+            sem(2 * groups, 2),
+            sem(2 * groups, 2),
+            sem(2 * groups),
         ],
         compiler_params=pltpu.CompilerParams(
             collective_id=2, has_side_effects=True, vmem_limit_bytes=60 * MIB

time: 1050 us -> 1010 us (0.962)
  Pallas kernels: 1000 us -> 971 us
    pallas_call x1, Pallas kernels: 524 us -> 479 us  [run_experts(): pl.pallas_call(functools.partial(experts_kernel, line, slots), out_shape=...]
where the time goes in v1:
time: 1010 us; the launch traced here: 1000 us
  Pallas kernels  971 us (96%)
  local copies, waits for them, and re-layouts  23.2 us (2%)
    pallas_call x1, Pallas kernels, run_experts(): pl.pallas_call(functools.partial(experts_kernel, line, slots), out_shape=...  479 us
    pallas_call x1, Pallas kernels, run_forward(): pl.pallas_call(functools.partial(forward_kernel, line, heads, kv_heads),...  205 us
    pallas_call x1, Pallas kernels, run_backward(): pl.pallas_call(functools.partial(backward_kernel, line, heads, kv_heads),...  163 us
    pallas_call x1, Pallas kernels, run_gradients(): pl.pallas_call(functools.partial(gradients_kernel, line), out_shape=(jax....  124 us

profile of v1, /device:TPU:26, one launch (start us, length us, event | category | flops | bytes accessed | tf_op | source)
XLA Modules:
  0.0 1003.9 jit_solution(9236111383357376524)
XLA Ops:
  0.7 1.3 broadcast_in_dim.49.gain1_ref
  2.0 1.3 broadcast_in_dim.50.gain2_ref
  3.3 0.7 fusion.7
  4.0 0.7 pad_maximum_fusion.3
  4.8 0.6 pad.4.picks_ref
  5.4 0.6 fusion.4
  5.9 0.8 pad_maximum_fusion.2
  6.8 2.0 pad_maximum_fusion.in_ref
  8.8 205.4 %shard_map.246 = (bf16[16,288,2048]{2,1,0:T(8,128)(2,1)}, bf16[2048,2560]{1,0:T(8,128)(2,1)}, bf16[2048,2048]{1,0:T(8,128)(2,1)}, f32[16,32,384]{2,1,0:T(8,128)}...) custom-call(bf16[2,144,2048]{2,1,0:T(8,128)(2,1)} %bitcast.49, ...), custom_call_target="tpu_custom_call" | custom-call | tf_op jit(solution)/shard_map/pallas_call | solution.py:1048
  214.2 1.2 fusion.3
  215.4 0.3 fusion
  215.7 0.3 compare_reduce_fusion
  216.1 0.2 convolution_select_fusion
  216.3 0.8 copy.40
  217.1 478.9 %shard_map.247 = (bf16[2,16,288,2048]{3,2,1,0:T(8,128)(2,1)}, bf16[1,16,288,2048]{3,2,1,0:T(8,128)(2,1)}, f32[2,2,144,2048]{3,2,1,0:T(8,128)}, bf16[2,3072,2048]...) custom-call(bf16[2,144,2048]{2,1,0:T(8,128)(2,1)} %get-tuple-element, ...), custom_call_target="tpu_custom_call" | custom-call | tf_op jit(solution)/shard_map/pallas_call | solution.py:2654
  696.0 162.7 %shard_map.248 = (bf16[2,144,2048]{2,1,0:T(8,128)(2,1)}, bf16[2,144,2048]{2,1,0:T(8,128)(2,1)}, bf16[2,288,2560]{2,1,0:T(8,128)(2,1)}, f32[2048,128]{1,0:T(8,128)}, f32[8,2048]{1,0:T(8,128)}) custom-call(bf16[2,144,2048]{2,1,0:T(8,128)(2,1)} %bitcast.44, f32[2,2,144,2048]{3,2,1,0:T(8,128)} %get-tuple-element.41.totals_ref, ...), custom_call_target="tpu_custom_call" | custom-call | tf_op jit(solution)/shard_map/pallas_call | solution.py:2039
  858.7 123.6 %shard_map.249 = (f32[128,2560]{1,0:T(8,128)}, f32[16,2,8,2048]{3,2,1,0:T(8,128)}, f32[2,2048,384]{2,1,0:T(8,128)}, f32[2,2048,384]{2,1,0:T(8,128)}, f32[2,384,2048]{2,1,0:T(8,128)}) custom-call(bf16[576,2048]{1,0:T(8,128)(2,1)} %bitcast.52, bf16[576,2560]{1,0:T(8,128)(2,1)} %bitcast.51, f32[8,2048]{1,0:T(8,128)} %get-tuple-element.51.gains_ref, ...), custom_call_target="tpu_custom_call" | custom-call | tf_op jit(solution)/shard_map/pallas_call | solution.py:2269
  982.3 1.9 reduce_sum.19
  984.2 0.5 slice_bitcast_fusion.1
  984.7 0.6 fusion.9
  985.3 1.8 fusion.8
  987.2 2.5 slice.34
  989.7 1.0 copy.58
  990.7 0.0 copy-done.1
  990.7 1.0 copy.59
  991.7 1.0 copy.60
  992.7 3.2 copy.61
  995.9 0.3 slice-done.3
  996.2 3.2 copy.62
  999.4 0.1 slice-done
  999.5 1.3 slice-done.1
  1000.8 2.7 copy.63
  (19 shorter events, 0.1 us)
Async XLA Ops:
  982.3 7.4 copy-start.2
  982.3 8.4 copy-start.1
  982.3 9.4 copy-start.3
  985.3 7.3 copy-start
  990.7 5.2 slice-start.2
  992.7 3.5 slice-start.3
  992.7 6.8 slice-start
  996.2 4.5 slice-start.1

commit v2 on v1

--- a/solution.py
+++ b/solution.py
@@ -999,10 +999,9 @@
         closing += [functools.partial(mix, i, *part) for part in parts(width)]
     closing += [functools.partial(close, i) for i in range(batch)]
     last = cots[0].steps()
-    mingle(opening + middle, steps_of([late] + cots, 1, last))
+    mingle(opening + middle, steps_of([late] + cots, 1, late.steps()))
     late_done()
-    for piece in closing:
-        piece()
+    mingle(closing, steps_of(cots, late.steps(), last))
 
     saves += [
         save(source, target, 2 + i)
@@ -1711,17 +1710,24 @@
     for copy in element_loads(0) + first_loads:
         copy.start()
 
-    def weight_load(ref, step):
-        slot = step % 2
+    out_steps, in_steps = out_ref.shape[0] // CHUNK, in_ref.shape[0] // CHUNK
+    stream = [(out_ref, step) for _ in range(batch) for step in range(out_steps)]
+    stream += [(in_ref, step) for _ in range(batch) for step in range(in_steps)]
+
+    def weight_load(index):
+        ref, step = stream[index]
         return pltpu.make_async_copy(
             rows_at(ref, step, CHUNK),
-            weight_rows.at[slot, :, pl.ds(0, ref.shape[1])],
-            row_sem.at[slot],
-        )
-
-    out_steps, in_steps = out_ref.shape[0] // CHUNK, in_ref.shape[0] // CHUNK
-    for step in range(2):
-        weight_load(out_ref, step).start()
+            weight_rows.at[index % 2, :, pl.ds(0, ref.shape[1])],
+            row_sem.at[index % 2],
+        )
+
+    def next_weights(index):
+        if index + 2 < len(stream):
+            weight_load(index + 2).start()
+
+    for index in range(2):
+        weight_load(index).start()
     gain_grads[...] = jnp.zeros_like(gain_grads)
     spot.greet()
     for copy in first_loads:
@@ -1762,23 +1768,22 @@
             for copy in element_loads(i + 1):
                 copy.start()
 
-    def hidden_done():
-        for i in range(batch):
-            hidden_copy(i).wait_send()
-            place = half_copy(hidden_grads, i, 1 - x)
-            spot.send(place, place, hidden_send.at[i], hidden_receive.at[i], CROSS).wait_recv()
-
-    def context_step(step):
-        weight_load(out_ref, step).wait()
-        columns = slice(step * CHUNK, (step + 1) * CHUNK)
-        context_grads[:, columns] = lax.dot_general(
-            hidden_grads[...],
-            weight_rows[step % 2, :, :width],
+    def hidden_done(i):
+        hidden_copy(i).wait_send()
+        place = half_copy(hidden_grads, i, 1 - x)
+        spot.send(place, place, hidden_send.at[i], hidden_receive.at[i], CROSS).wait_recv()
+
+    def context_step(i, step):
+        index = i * out_steps + step
+        weight_load(index).wait()
+        rows = slice(i * length, (i + 1) * length)
+        context_grads[rows, step * CHUNK : (step + 1) * CHUNK] = lax.dot_general(
+            hidden_grads[rows],
+            weight_rows[index % 2, :, :width],
             TRANSPOSED_RIGHT,
             preferred_element_type=jnp.float32,
         ).astype(jnp.bfloat16)
-        if step + 2 < out_steps:
-            weight_load(out_ref, step + 2).start()
+        next_weights(index)
 
     def out_step(step):
         columns = slice(step * CHUNK, (step + 1) * CHUNK)
@@ -1802,15 +1807,9 @@
         tree_receive,
     )
 
-    def in_start():
-        for step in range(2):
-            weight_load(in_ref, step).start()
-
     def tree_start():
         for z in range(line):
             tree.begin(z)
-        for copy in head_loads(0):
-            copy.start()
 
     def turns():
         return [(i, shared) for i in range(batch) for shared in range(kv_heads)]
@@ -1947,16 +1946,17 @@
         for i in range(batch)
     ]
 
-    def normed_step(step):
-        weight_load(in_ref, step).wait()
-        normed_grads[:, step * CHUNK : (step + 1) * CHUNK] = lax.dot_general(
-            grads[...],
-            weight_rows[step % 2],
+    def normed_step(i, step):
+        index = batch * out_steps + i * in_steps + step
+        weight_load(index).wait()
+        rows = slice(i * length, (i + 1) * length)
+        normed_grads[rows, step * CHUNK : (step + 1) * CHUNK] = lax.dot_general(
+            grads[rows],
+            weight_rows[index % 2],
             TRANSPOSED_RIGHT,
             preferred_element_type=jnp.float32,
         ).astype(jnp.bfloat16)
-        if step + 2 < in_steps:
-            weight_load(in_ref, step + 2).start()
+        next_weights(index)
 
     def normed_copy(i):
         return spot.send(
@@ -1988,15 +1988,28 @@
         add_rows(result.at[i], [kept.at[i]])
         result_save(i, input_grad).start()
 
-    opening = [functools.partial(element_rows, i) for i in range(batch)] + [hidden_done]
-    opening += [functools.partial(out_step, step) for step in range(out_steps)]
-    opening += [tree_start, functools.partial(context_step, 0), tree.cross]
-    opening += [functools.partial(context_step, step) for step in range(1, out_steps)]
-    opening.append(in_start)
-    attending = [piece for index in range(len(turns())) for piece in attend_pieces(index)]
-    closing = attending + [copy.start for copy in saves]
-    closing += [functools.partial(normed_step, step) for step in range(in_steps)]
-    closing += [normed_copy(i).start for i in range(batch)]
+    for copy in head_loads(0):
+        copy.start()
+    attending = [attend_pieces(index) for index in range(len(turns()))]
+    contexts = [
+        [functools.partial(context_step, i, step) for step in range(out_steps)]
+        for i in range(batch)
+    ]
+    opening = [functools.partial(element_rows, i) for i in range(batch)]
+    opening += attending[0][:1] + [functools.partial(hidden_done, 0)] + contexts[0]
+    opening += [functools.partial(hidden_done, i) for i in range(1, batch)]
+    opening += [functools.partial(out_step, step) for step in range(out_steps)] + [tree_start]
+    for steps in contexts[1:]:
+        opening += steps
+    opening.append(tree.cross)
+    closing = []
+    for index in range(len(turns())):
+        i = turns()[index][0]
+        closing += attending[index][0 if index else 1 :]
+        if index + 1 == len(turns()) or turns()[index + 1][0] > i:
+            closing += [saves[i].start]
+            closing += [functools.partial(normed_step, i, step) for step in range(in_steps)]
+            closing += [lambda i=i: normed_copy(i).start()]
     closing += [functools.partial(input_rows, i) for i in range(batch)]
     for piece in opening:
         piece()
@@ -2187,8 +2200,14 @@
     )
     chunk = PLANE * depth
 
+    def far_first(step):
+        z = narrow.z
+        down = jnp.where(line - 1 - step > z, line - 1 - step, line - 2 - step)
+        up = jnp.where(step < z, step, step + 1)
+        return jnp.where(step == line - 1, z, jnp.where(2 * z < line, down, up))
+
     def plane(step, _):
-        z = lax.rem(narrow.z + 1 + step, line)
+        z = far_first(step)
         columns = pl.ds(pl.multiple_of(z * chunk, LANES), chunk)
         for start in range(0, width, CHUNK):
             parts[pl.ds(pl.multiple_of(z * chunk, 16), chunk), start : start + CHUNK] = (
@@ -2200,9 +2219,11 @@
                 ).astype(jnp.bfloat16)
             )
         tree.begin(z)
+        when(step > 0, lambda: tree.to_first(far_first(step - 1)))
         return 0
 
     lax.fori_loop(0, line, plane, 0)
+    tree.to_first(narrow.z)
 
     def piece(index):
         expert, kind, turn = pieces[index]
@@ -2239,7 +2260,6 @@
             for copy in saves(expert, kind):
                 copy.start()
 
-    tree.cross()
     work = tree.tasks()
     steps = list(range(1, gains.steps()))
     filler = list(range(len(pieces)))

time: 1010 us -> 997 us (0.987)
  Pallas kernels: 971 us -> 954 us
    pallas_call x1, Pallas kernels: 163 us -> 151 us  [run_backward(): pl.pallas_call(functools.partial(backward_kernel, line, heads, kv_heads),...]
where the time goes in v2:
time: 997 us; the launch traced here: 988 us
  Pallas kernels  954 us (96%)
  local copies, waits for them, and re-layouts  23.2 us (2%)
    pallas_call x1, Pallas kernels, run_experts(): pl.pallas_call(functools.partial(experts_kernel, line, slots), out_shape=...  476 us
    pallas_call x1, Pallas kernels, run_forward(): pl.pallas_call(functools.partial(forward_kernel, line, heads, kv_heads),...  204 us
    pallas_call x1, Pallas kernels, run_backward(): pl.pallas_call(functools.partial(backward_kernel, line, heads, kv_heads),...  151 us
    pallas_call x1, Pallas kernels, run_gradients(): pl.pallas_call(functools.partial(gradients_kernel, line), out_shape=(jax....  123 us

profile of v2, /device:TPU:26, one launch (start us, length us, event | category | flops | bytes accessed | tf_op | source)
XLA Modules:
  0.0 987.7 jit_solution(6575212998353327281)
XLA Ops:
  0.7 1.3 broadcast_in_dim.49.gain1_ref
  2.0 1.3 broadcast_in_dim.50.gain2_ref
  3.3 0.7 fusion.7
  4.0 0.7 pad_maximum_fusion.3
  4.8 0.6 pad.4.picks_ref
  5.4 0.6 fusion.4
  5.9 0.8 pad_maximum_fusion.2
  6.8 2.0 pad_maximum_fusion.in_ref
  8.8 204.2 %shard_map.246 = (bf16[16,288,2048]{2,1,0:T(8,128)(2,1)}, bf16[2048,2560]{1,0:T(8,128)(2,1)}, bf16[2048,2048]{1,0:T(8,128)(2,1)}, f32[16,32,384]{2,1,0:T(8,128)}...) custom-call(bf16[2,144,2048]{2,1,0:T(8,128)(2,1)} %bitcast.49, ...), custom_call_target="tpu_custom_call" | custom-call | tf_op jit(solution)/shard_map/pallas_call | solution.py:1047
  213.0 1.2 fusion.3
  214.2 0.3 fusion
  214.5 0.3 compare_reduce_fusion
  214.9 0.2 convolution_select_fusion
  215.1 0.8 copy.40
  215.8 475.6 %shard_map.247 = (bf16[2,16,288,2048]{3,2,1,0:T(8,128)(2,1)}, bf16[1,16,288,2048]{3,2,1,0:T(8,128)(2,1)}, f32[2,2,144,2048]{3,2,1,0:T(8,128)}, bf16[2,3072,2048]...) custom-call(bf16[2,144,2048]{2,1,0:T(8,128)(2,1)} %get-tuple-element, ...), custom_call_target="tpu_custom_call" | custom-call | tf_op jit(solution)/shard_map/pallas_call | solution.py:2674
  691.5 151.4 %shard_map.248 = (bf16[2,144,2048]{2,1,0:T(8,128)(2,1)}, bf16[2,144,2048]{2,1,0:T(8,128)(2,1)}, bf16[2,288,2560]{2,1,0:T(8,128)(2,1)}, f32[2048,128]{1,0:T(8,128)}, f32[8,2048]{1,0:T(8,128)}) custom-call(bf16[2,144,2048]{2,1,0:T(8,128)(2,1)} %bitcast.44, f32[2,2,144,2048]{3,2,1,0:T(8,128)} %get-tuple-element.41.totals_ref, ...), custom_call_target="tpu_custom_call" | custom-call | tf_op jit(solution)/shard_map/pallas_call | solution.py:2052
  842.9 123.2 %shard_map.249 = (f32[128,2560]{1,0:T(8,128)}, f32[16,2,8,2048]{3,2,1,0:T(8,128)}, f32[2,2048,384]{2,1,0:T(8,128)}, f32[2,2048,384]{2,1,0:T(8,128)}, f32[2,384,2048]{2,1,0:T(8,128)}) custom-call(bf16[576,2048]{1,0:T(8,128)(2,1)} %bitcast.52, bf16[576,2560]{1,0:T(8,128)(2,1)} %bitcast.51, f32[8,2048]{1,0:T(8,128)} %get-tuple-element.51.gains_ref, ...), custom_call_target="tpu_custom_call" | custom-call | tf_op jit(solution)/shard_map/pallas_call | solution.py:2289
  966.1 0.0 copy-start.2
  966.1 1.9 reduce_sum.19
  967.9 0.5 slice_bitcast_fusion.1
  968.5 0.6 fusion.9
  969.1 1.8 fusion.8
  970.9 2.5 slice.34
  973.4 1.0 copy.58
  974.4 1.0 copy.59
  975.4 1.0 copy.60
  976.4 3.2 copy.61
  979.6 0.3 slice-done.3
  980.0 3.2 copy.62
  983.2 0.1 slice-done
  983.3 1.3 slice-done.1
  984.5 2.7 copy.63
  (19 shorter events, 0.1 us)
Async XLA Ops:
  966.1 7.4 copy-start.2
  966.1 8.4 copy-start.1
  966.1 9.4 copy-start.3
  969.1 7.3 copy-start
  974.4 5.2 slice-start.2
  976.4 3.5 slice-start.3
  976.4 6.8 slice-start
  980.0 4.5 slice-start.1

commit v3 on v2

--- a/solution.py
+++ b/solution.py
@@ -851,6 +851,7 @@
     early, late = weights[:2], weights[2]
     for tree in early:
         tree.begin()
+    late.begin()
 
     def token_copies(i):
         place = rows_at(tokens.at[i], x, half)
@@ -868,7 +869,6 @@
         return 0
 
     lax.fori_loop(1, late.steps(), steps, 0)
-    late.begin()
     for tree in cots:
         tree.begin()
     for i in range(batch):
@@ -1999,9 +1999,9 @@
     opening += attending[0][:1] + [functools.partial(hidden_done, 0)] + contexts[0]
     opening += [functools.partial(hidden_done, i) for i in range(1, batch)]
     opening += [functools.partial(out_step, step) for step in range(out_steps)] + [tree_start]
-    for steps in contexts[1:]:
+    opening += contexts[1][:1] + [tree.cross] + contexts[1][1:]
+    for steps in contexts[2:]:
         opening += steps
-    opening.append(tree.cross)
     closing = []
     for index in range(len(turns())):
         i = turns()[index][0]

time: 997 us -> 997 us (level)
  no operation moved by 1% of the time
where the time goes in v3:
time: 997 us; the launch traced here: 984 us
  Pallas kernels  950 us (95%)
  local copies, waits for them, and re-layouts  23.2 us (2%)
    pallas_call x1, Pallas kernels, run_experts(): pl.pallas_call(functools.partial(experts_kernel, line, slots), out_shape=...  476 us
    pallas_call x1, Pallas kernels, run_forward(): pl.pallas_call(functools.partial(forward_kernel, line, heads, kv_heads),...  204 us
    pallas_call x1, Pallas kernels, run_backward(): pl.pallas_call(functools.partial(backward_kernel, line, heads, kv_heads),...  157 us
    pallas_call x1, Pallas kernels, run_gradients(): pl.pallas_call(functools.partial(gradients_kernel, line), out_shape=(jax....  114 us

profile of v3, /device:TPU:26, one launch (start us, length us, event | category | flops | bytes accessed | tf_op | source)
XLA Modules:
  0.0 983.6 jit_solution(8805939608229626839)
XLA Ops:
  0.7 1.3 broadcast_in_dim.49.gain1_ref
  2.0 1.3 broadcast_in_dim.50.gain2_ref
  3.3 0.7 fusion.7
  4.0 0.7 pad_maximum_fusion.3
  4.8 0.6 pad.4.picks_ref
  5.4 0.6 fusion.4
  5.9 0.8 pad_maximum_fusion.2
  6.8 2.0 pad_maximum_fusion.in_ref
  8.8 204.2 %shard_map.246 = (bf16[16,288,2048]{2,1,0:T(8,128)(2,1)}, bf16[2048,2560]{1,0:T(8,128)(2,1)}, bf16[2048,2048]{1,0:T(8,128)(2,1)}, f32[16,32,384]{2,1,0:T(8,128)}...) custom-call(bf16[2,144,2048]{2,1,0:T(8,128)(2,1)} %bitcast.49, ...), custom_call_target="tpu_custom_call" | custom-call | tf_op jit(solution)/shard_map/pallas_call | solution.py:1047
  213.0 1.2 fusion.3
  214.2 0.3 fusion
  214.5 0.3 compare_reduce_fusion
  214.9 0.2 convolution_select_fusion
  215.1 0.8 copy.40
  215.8 475.6 %shard_map.247 = (bf16[2,16,288,2048]{3,2,1,0:T(8,128)(2,1)}, bf16[1,16,288,2048]{3,2,1,0:T(8,128)(2,1)}, f32[2,2,144,2048]{3,2,1,0:T(8,128)}, bf16[2,3072,2048]...) custom-call(bf16[2,144,2048]{2,1,0:T(8,128)(2,1)} %get-tuple-element, ...), custom_call_target="tpu_custom_call" | custom-call | tf_op jit(solution)/shard_map/pallas_call | solution.py:2674
  691.5 156.7 %shard_map.248 = (bf16[2,144,2048]{2,1,0:T(8,128)(2,1)}, bf16[2,144,2048]{2,1,0:T(8,128)(2,1)}, bf16[2,288,2560]{2,1,0:T(8,128)(2,1)}, f32[2048,128]{1,0:T(8,128)}, f32[8,2048]{1,0:T(8,128)}) custom-call(bf16[2,144,2048]{2,1,0:T(8,128)(2,1)} %bitcast.44, f32[2,2,144,2048]{3,2,1,0:T(8,128)} %get-tuple-element.41.totals_ref, ...), custom_call_target="tpu_custom_call" | custom-call | tf_op jit(solution)/shard_map/pallas_call | solution.py:2052
  848.2 113.7 %shard_map.249 = (f32[128,2560]{1,0:T(8,128)}, f32[16,2,8,2048]{3,2,1,0:T(8,128)}, f32[2,2048,384]{2,1,0:T(8,128)}, f32[2,2048,384]{2,1,0:T(8,128)}, f32[2,384,2048]{2,1,0:T(8,128)}) custom-call(bf16[576,2048]{1,0:T(8,128)(2,1)} %bitcast.52, bf16[576,2560]{1,0:T(8,128)(2,1)} %bitcast.51, f32[8,2048]{1,0:T(8,128)} %get-tuple-element.51.gains_ref, ...), custom_call_target="tpu_custom_call" | custom-call | tf_op jit(solution)/shard_map/pallas_call | solution.py:2289
  962.0 1.9 reduce_sum.19
  963.9 0.5 slice_bitcast_fusion.1
  964.4 0.6 fusion.9
  965.0 1.8 fusion.8
  966.8 2.5 slice.34
  969.3 1.0 copy.58
  970.3 0.0 copy-done.1
  970.3 1.0 copy.59
  971.4 1.0 copy.60
  972.3 3.2 copy.61
  975.5 0.3 slice-done.3
  975.9 3.2 copy.62
  979.1 0.1 slice-done
  979.2 1.3 slice-done.1
  980.4 2.7 copy.63
  (19 shorter events, 0.1 us)
Async XLA Ops:
  962.0 7.4 copy-start.2
  962.0 8.4 copy-start.1
  962.0 9.4 copy-start.3
  965.0 7.3 copy-start
  970.3 5.2 slice-start.2
  972.3 3.5 slice-start.3
  972.3 6.8 slice-start
  975.9 4.5 slice-start.1
